TPU v7x, 512 devices: a whole 4x8x8 slice. The times are simulated.
512 devices in a mesh: gx: 16 (over z, core), gy: 32 (over x, y).
Axes of the slice: x: 4, y: 8, z: 8, core: 2. Of those that a mesh axis runs over, the one named last changes fastest.
Arguments:
- features: bfloat16 [524288, 768], P(('gx', 'gy')), may hold values from -12 to 12
- hidden_weight: bfloat16 [768, 1024], replicated, may hold values from -0.21875 to 0.21875
- class_weight: bfloat16 [1024, 153], replicated, may hold values from -0.1875 to 0.1875
- req_owner: int32 [512, 3072, 1], P(('gx', 'gy')), may hold values from 0 to 511; in each aligned block of 3072 rows (0 to 3071, 3072 to 6143, ..., all dimensions but the last counted through in order) at most 12 rows name the same one
- req_block: int32 [512, 3072], P(('gx', 'gy')), may hold values from 0 to 7
- req_offset: int32 [512, 3072], P(('gx', 'gy')), may hold values from 0 to 127
- hop1_counts: int32 [512, 256], P(('gx', 'gy')), may hold values from 1 to 6, 512 in all within a row
- hop2_counts: int32 [512, 768], P(('gx', 'gy')), may hold values from 1 to 8, 2304 in all within a row
- prior_agg: bfloat16 [393216, 768], P(('gx', 'gy')), may hold values from -6 to 6
- prior_hop1: int32 [512, 256], P(('gx', 'gy')), may hold values from 1 to 6, 512 in all within a row
- cotangent: bfloat16 [131072, 153], P(('gx', 'gy')), may hold values from -0.119628906 to 0.119628906
Outputs:
- logits: float32 [131072, 153], P(('gx', 'gy'))
- hidden_grad: float32 [768, 1024], P(None, ('gx', 'gy'))
- class_grad: float32 [1024, 153], replicated
Inputs may be any that keep to these rules, and one draw needn't show every extreme that they name: `req_owner`: among the 3072 reads of one device, no owner is named more than 12 times, a bound that some block reaches. `hop1_counts`: each device's row sums to 512. `hop2_counts`: each device's row sums to 2304. `prior_hop1`: each device's row sums to 512.
All inputs are finite; a program needn't handle non-finite values.
Results may differ from a plain program's by a relative error of at most 0.0048.
Values may be sent and summed in bfloat16 or wider, within the bound.
No kernel may reach another device: no remote copies, remote signals or barrier semaphores. Data moves between devices by JAX's collectives and lax.ppermute only.
A program may use at most 128 MiB of HBM per device.

v0:
```python
import jax
import jax.numpy as jnp
from jax import lax
from jax.sharding import PartitionSpec as P

BLOCK_ROWS = 128


def segment_ids(counts, total):
    ends = jnp.cumsum(counts)
    positions = jnp.arange(total, dtype=jnp.int32)
    return jnp.searchsorted(ends, positions, side="right")


def second_layer(agg_one, hop1_counts, hidden_weight):
    nodes = agg_one.shape[0]
    seeds = hop1_counts.shape[0]
    pre_act = jnp.dot(agg_one, hidden_weight, preferred_element_type=jnp.float32)
    sigma = jax.nn.sigmoid(pre_act)
    hidden = (pre_act * sigma).astype(jnp.bfloat16)
    hop1_ids = segment_ids(hop1_counts, nodes - seeds)
    scale_two = 1.0 / (1.0 + hop1_counts.astype(jnp.float32))
    summed_two = jax.ops.segment_sum(
        hidden[seeds:].astype(jnp.float32), hop1_ids, num_segments=seeds
    )
    agg_two = ((hidden[:seeds].astype(jnp.float32) + summed_two) * scale_two[:, None]).astype(
        jnp.bfloat16
    )
    return (pre_act, sigma, hop1_ids, scale_two, agg_two)


def forward_pass(fetched, hop1_counts, hop2_counts, hidden_weight, class_weight):
    nodes = hop2_counts.shape[0]
    hop2_ids = segment_ids(hop2_counts, fetched.shape[0] - nodes)
    summed = jax.ops.segment_sum(fetched[nodes:].astype(jnp.float32), hop2_ids, num_segments=nodes)
    agg_one = (
        (fetched[:nodes].astype(jnp.float32) + summed)
        / (1.0 + hop2_counts.astype(jnp.float32))[:, None]
    ).astype(jnp.bfloat16)
    agg_two = second_layer(agg_one, hop1_counts, hidden_weight)[4]
    return jnp.dot(agg_two, class_weight, preferred_element_type=jnp.float32)


def backward_pass(prior_agg, prior_hop1, cotangent, hidden_weight, class_weight):
    pre_act, sigma, hop1_ids, scale_two, agg_two = second_layer(
        prior_agg, prior_hop1, hidden_weight
    )
    class_term = lax.dot_general(
        agg_two, cotangent, (((0,), (0,)), ((), ())), preferred_element_type=jnp.float32
    )
    d_agg = (
        lax.dot_general(
            cotangent, class_weight, (((1,), (1,)), ((), ())), preferred_element_type=jnp.float32
        )
        * scale_two[:, None]
    )
    d_hidden = jnp.concatenate([d_agg, d_agg[hop1_ids]], axis=0)
    d_pre = (d_hidden * sigma * (1.0 + pre_act * (1.0 - sigma))).astype(jnp.bfloat16)
    hidden_term = lax.dot_general(
        prior_agg, d_pre, (((0,), (0,)), ((), ())), preferred_element_type=jnp.float32
    )
    return (class_term, hidden_term)


def on_device(
    features,
    hidden_weight,
    class_weight,
    req_owner,
    req_block,
    req_offset,
    hop1_counts,
    hop2_counts,
    prior_agg,
    prior_hop1,
    cotangent,
):
    outer = lax.axis_size("gx")
    inner = lax.axis_size("gy")
    devices = outer * inner
    owners = req_owner.reshape(-1)
    wanted = (req_block * BLOCK_ROWS + req_offset).reshape(-1)
    requests = owners.shape[0]
    capacity = 2 * requests // devices
    sorted_pos = jnp.argsort(owners, stable=True)
    sorted_own = owners[sorted_pos]
    first_pos = jnp.searchsorted(sorted_own, jnp.arange(devices, dtype=jnp.int32), side="left")
    rank_sorted = jnp.arange(requests, dtype=jnp.int32) - first_pos[sorted_own]
    slot_of = (
        jnp.zeros((requests,), jnp.int32).at[sorted_pos].set(sorted_own * capacity + rank_sorted)
    )
    outgoing = (
        jnp.zeros((devices * capacity,), jnp.int32)
        .at[slot_of]
        .set(wanted)
        .reshape(outer, inner, capacity)
    )
    incoming = lax.all_to_all(
        lax.all_to_all(outgoing, "gx", split_axis=0, concat_axis=0, tiled=True),
        "gy",
        split_axis=1,
        concat_axis=1,
        tiled=True,
    )
    answers = features[incoming]
    returned = lax.all_to_all(
        lax.all_to_all(answers, "gx", split_axis=0, concat_axis=0, tiled=True),
        "gy",
        split_axis=1,
        concat_axis=1,
        tiled=True,
    )
    class_term, hidden_term = backward_pass(
        prior_agg, prior_hop1.reshape(-1), cotangent, hidden_weight, class_weight
    )
    hidden_grad = lax.psum_scatter(hidden_term, ("gx", "gy"), scatter_dimension=1, tiled=True)
    class_grad = lax.psum(class_term, ("gx", "gy"))
    fetched = returned.reshape(devices * capacity, features.shape[1])[slot_of]
    logits = forward_pass(
        fetched, hop1_counts.reshape(-1), hop2_counts.reshape(-1), hidden_weight, class_weight
    )
    return (logits, hidden_grad, class_grad)


def solution(mesh):
    placed = (
        P(("gx", "gy"), None),
        P(),
        P(),
        P(("gx", "gy"), None, None),
        P(("gx", "gy"), None),
        P(("gx", "gy"), None),
        P(("gx", "gy"), None),
        P(("gx", "gy"), None),
        P(("gx", "gy"), None),
        P(("gx", "gy"), None),
        P(("gx", "gy"), None),
    )
    return jax.shard_map(
        on_device,
        mesh=mesh,
        in_specs=placed,
        out_specs=(P(("gx", "gy"), None), P(None, ("gx", "gy")), P()),
        check_vma=False,
    )
```

profile of v0, /device:TPU:16, one launch (start us, length us, event | category | flops | bytes accessed | tf_op | source)
XLA Modules:
  0.0 937.6 jit_solution(16344774710306744180)
XLA Ops:
  13.8 17.4 %gather_fusion.4 = s32[3072]{0:T(1024)S(1)} fusion(s32[3072]{0:T(1024)S(1)} %bitcast.31, s32[3072]{0:T(1024)S(1)} %get-tuple-element.371), kind=kCustom, calls=%fused_computation.4 | custom fusion | bytes 36864 | tf_op jit(solution)/shard_map/gather | solution.py:86
  31.3 38.9 %while.85 = (s32[]{:T(128)}, u32[512]{0:T(512)S(1)}, u32[512]{0:T(512)S(1)}, s32[3072]{0:T(1024)S(1)}, s32[]{:T(128)}, /*index=5*/s32[]{:T(128)}, s32[]{}) while((s32[]{:T(128)}, u32[512]{0:T(512)S(1)}, u32[512]{0:T(512)S(1)}, s32[3072]{0:T(1024)S(1)}, s32[]{:T(128)}, /*index=5*/s32[]{:T(128)}, s32[]{}) %tuple.123), condition=%wide.region_2.3_spmd.clone, body=%wide.region_1.2_spmd.clone.sunk | while | flops 10244 | bytes 37989 | solution.py:87
  70.2 19.5 %gather_fusion.5 = s32[3072]{0:T(1024)S(1)} fusion(s32[512]{0:T(512)S(1)} %convert_element_type.94, s32[3072]{0:T(1024)S(1)} %broadcast_clamp_fusion.2), kind=kCustom, calls=%fused_computation.5 | custom fusion | bytes 36864 | tf_op jit(solution)/shard_map/gather | solution.py:88
  89.7 11.8 %scatter_custom_fusion = s32[3072]{0:T(1024)S(1)} fusion(s32[3072]{0:T(1024)S(1)} %get-tuple-element.372, s32[3072]{0:T(1024)S(1)} %subtract_add_fusion, s32[]{:T(128)} %constant.123.clone.1), kind=kCustom, calls=%fused_computation.79 | custom fusion | bytes 12292 | tf_op jit(solution)/shard_map/scatter | solution.py:90
  101.6 11.8 %scatter_custom_fusion.1 = s32[6144]{0:T(1024)S(1)} fusion(s32[3072]{0:T(1024)S(1)} %get-tuple-element.370, s32[3072]{0:T(1024)S(1)} %bitcast.38, s32[]{:T(128)} %constant.123.clone.1), kind=kCustom, calls=%fused_computation.74 | custom fusion | bytes 24580 | tf_op jit(solution)/shard_map/scatter | solution.py:95
  114.0 17.9 %all_to_all.20 = s32[16,1,384]{2,1,0:T(1,128)S(1)} all-to-all(s32[16,1,384]{2,1,0:T(1,128)S(1)} %reshape.275), channel_id=1, replica_groups=mesh['gx'=16,'gy'=32] {'gx'}, dimensions={0} | all-to-all | bytes 49152 | tf_op jit(solution)/shard_map/all_to_all | solution.py:99
  133.6 17.8 %all_to_all.21 = s32[32,1,192]{2,1,0:T(1,128)S(1)} all-to-all(s32[32,1,192]{2,1,0:T(1,128)S(1)} %reshape.277), channel_id=1, replica_groups=mesh['gx'=16,'gy'=32] {'gy'}, dimensions={0} | all-to-all | bytes 49152 | tf_op jit(solution)/shard_map/all_to_all | solution.py:98
  152.6 26.1 %gather_fusion.6 = bf16[6144,768]{1,0:T(8,128)(2,1)} fusion(bf16[1024,768]{1,0:T(8,128)(2,1)S(1)} %copy-done, s32[6144]{0:T(1024)S(1)} %broadcast_clamp_fusion), kind=kCustom, calls=%fused_computation.6 | custom fusion | bytes 18898944 | tf_op jit(solution)/shard_map/gather | solution.py:105
  178.8 15.3 %reshape.171 = bf16[16,32,12,768]{3,2,1,0:T(8,128)(2,1)} reshape(bf16[6144,768]{1,0:T(8,128)(2,1)} %gather_fusion.6) | data formatting | bytes 18874368 | tf_op jit(solution)/shard_map/gather | solution.py:105
  194.1 12.2 %copy.17 = bf16[16,32,12,768]{3,1,2,0:T(8,128)(2,1)} copy(bf16[16,32,12,768]{3,2,1,0:T(8,128)(2,1)} %reshape.171) | data formatting | bytes 18874368 | tf_op jit(solution)/shard_map/gather | solution.py:105
  212.1 32.4 %while.88 = (s32[]{:T(128)}, u32[512]{0:T(512)S(1)}, u32[512]{0:T(512)S(1)}, s32[256]{0:T(256)S(1)}, s32[]{:T(128)}, /*index=5*/s32[]{:T(128)}, s32[]{}) while((s32[]{:T(128)}, u32[512]{0:T(512)S(1)}, u32[512]{0:T(512)S(1)}, s32[256]{0:T(256)S(1)}, s32[]{:T(128)}, /*index=5*/s32[]{:T(128)}, s32[]{}) %tuple.132), condition=%wide.region_18.19_spmd.clone, body=%wide.region_17.18_spmd.clone.sunk | while | flops 10244 | bytes 37989 | solution.py:12
  244.5 173.6 %all-to-all-done.2 = bf16[16,32,12,768]{3,1,2,0:T(8,128)(2,1)} async-done(((bf16[16,32,12,768]{3,1,2,0:T(8,128)(2,1)}), bf16[16,32,12,768]{3,1,2,0:T(8,128)(2,1)}, u32[]{:S(2)}, u32[]{:S(2)}) %all-to-all-start.2) | async-done | bytes 9437216 | tf_op jit(solution)/shard_map/all_to_all | solution.py:107
  418.0 12.6 %copy.18 = bf16[16,32,12,768]{3,0,2,1:T(8,128)(2,1)} copy(bf16[16,32,12,768]{3,1,2,0:T(8,128)(2,1)} %all-to-all-done.2) | data formatting | bytes 18874368 | tf_op jit(solution)/shard_map/all_to_all | solution.py:107
  460.5 86.0 %while.86 = (s32[]{:T(128)}, u32[2304]{0:T(1024)S(1)}, u32[2304]{0:T(1024)S(1)}, s32[768]{0:T(1024)S(1)}, s32[]{:T(128)}, /*index=5*/s32[]{:T(128)}, s32[]{}) while((s32[]{:T(128)}, u32[2304]{0:T(1024)S(1)}, u32[2304]{0:T(1024)S(1)}, s32[768]{0:T(1024)S(1)}, s32[]{:T(128)}, /*index=5*/s32[]{:T(128)}, s32[]{}) %tuple.126), condition=%wide.region_8.9_spmd.clone, body=%wide.region_7.8_spmd.clone.sunk | while | flops 44548 | bytes 164453 | solution.py:12
  460.5 8.5 gather_fusion.1
  469.1 8.5 gather_fusion.1
  477.7 8.5 gather_fusion.1
  486.3 8.5 gather_fusion.1
  546.5 32.4 %while.87 = (s32[]{:T(128)}, u32[512]{0:T(512)S(1)}, u32[512]{0:T(512)S(1)}, s32[256]{0:T(256)S(1)}, s32[]{:T(128)}, /*index=5*/s32[]{:T(128)}, s32[]{}) while((s32[]{:T(128)}, u32[512]{0:T(512)S(1)}, u32[512]{0:T(512)S(1)}, s32[256]{0:T(256)S(1)}, s32[]{:T(128)}, /*index=5*/s32[]{:T(128)}, s32[]{}) %tuple.129), condition=%wide.region_13.14_spmd.clone, body=%wide.region_12.13_spmd.clone.sunk | while | flops 10244 | bytes 37989 | solution.py:12
  579.0 265.8 %all-reduce.4.cloned.1.call-done = (f32[768,1024]{0,1:T(8,128)}, f32[1024,153]{0,1:T(8,128)}) async-done(((f32[768,1024]{0,1:T(8,128)}, f32[1024,153]{0,1:T(8,128)}), (f32[768,1024]{0,1:T(8,128)}, f32[1024,153]{0,1:T(8,128)})) %all-reduce.4.cloned.1.call-update) | async-done | bytes 3772432
  846.2 10.8 %copy.19 = bf16[16,32,12,768]{3,2,1,0:T(8,128)(2,1)} copy(bf16[16,32,12,768]{3,0,2,1:T(8,128)(2,1)} %all-to-all-done.3) | data formatting | bytes 18874368 | tf_op jit(solution)/shard_map/all_to_all | solution.py:106
  857.0 15.4 %reshape.115 = bf16[6144,768]{1,0:T(8,128)(2,1)} reshape(bf16[16,32,12,768]{3,2,1,0:T(8,128)(2,1)} %copy.19) | data formatting | bytes 18874368 | tf_op jit(solution)/shard_map/reshape | solution.py:118
  872.4 19.4 %gather_fusion.7 = bf16[3072,768]{1,0:T(8,128)(2,1)} fusion(bf16[6144,768]{1,0:T(8,128)(2,1)} %reshape.115, s32[3072]{0:T(1024)S(1)} %get-tuple-element.369), kind=kCustom, calls=%fused_computation.7 | custom fusion | bytes 9449472 | tf_op jit(solution)/shard_map/gather | solution.py:118
  894.7 21.3 %scatter_custom_fusion.2 = f32[768,768]{1,0:T(8,128)} fusion(f32[768,768]{1,0:T(8,128)} %slice_convert_fusion, s32[2304]{0:T(1024)S(1)} %convert_element_type.96, bf16[3072,768]{1,0:T(8,128)(2,1)} %gather_fusion.7), kind=kCustom, calls=%fused_computation.38 | custom fusion | flops 3538944 | bytes 5898240 | tf_op jit(solution)/shard_map/scatter-add | solution.py:35
  (334 shorter events, 217.4 us)
Async XLA Ops:
  7.2 145.5 %copy-start = (bf16[1024,768]{1,0:T(8,128)(2,1)S(1)}, bf16[1024,768]{1,0:T(8,128)(2,1)}, u32[]{:S(2)}) copy-start(bf16[1024,768]{1,0:T(8,128)(2,1)} %param.19) | copy-start | bytes 4718596
  7.2 6.6 copy-start.2
  70.1 31.4 %copy-start.7 = (s32[1,3072]{1,0:T(1,128)S(1)}, s32[1,3072]{1,0:T(1,128)}, u32[]{:S(2)}) copy-start(s32[1,3072]{1,0:T(1,128)} %param.24) | copy-start | bytes 36868
  70.1 31.4 %copy-start.8 = (s32[1,3072]{1,0:T(1,128)S(1)}, s32[1,3072]{1,0:T(1,128)}, u32[]{:S(2)}) copy-start(s32[1,3072]{1,0:T(1,128)} %param.23) | copy-start | bytes 36868
  206.3 5.1 copy-start.9
  206.3 211.7 %all-to-all-start.2 = ((bf16[16,32,12,768]{3,1,2,0:T(8,128)(2,1)}), bf16[16,32,12,768]{3,1,2,0:T(8,128)(2,1)}, u32[]{:S(2)}, u32[]{:S(2)}) async-start(bf16[16,32,12,768]{3,1,2,0:T(8,128)(2,1)} %copy.17), calls=%async_computation.2 | async-start | bytes 18874368 | tf_op jit(solution)/shard_map/all_to_all | solution.py:107
  430.6 6.9 copy-start.11
  430.6 415.5 %all-to-all-start.3 = ((bf16[16,32,12,768]{3,0,2,1:T(8,128)(2,1)}), bf16[16,32,12,768]{3,0,2,1:T(8,128)(2,1)}, u32[]{:S(2)}, u32[]{:S(2)}) async-start(bf16[16,32,12,768]{3,0,2,1:T(8,128)(2,1)} %copy.18), calls=%async_computation.3 | async-start | bytes 18874368 | tf_op jit(solution)/shard_map/all_to_all | solution.py:106
  437.5 407.3 %all-reduce.4.cloned.1.call-start = ((), (), s32[]{:S(2)}) async-start(), calls=%async_computation.4 | async-start | bytes 7602176
  442.2 5.6 copy-start.4
  442.2 5.6 copy-start.5
  458.6 0.7 copy-start.6
  458.6 1.1 copy-start.10
  916.0 14.2 %copy-start.1 = (bf16[1024,768]{1,0:T(8,128)(2,1)S(1)}, bf16[1024,768]{1,0:T(8,128)(2,1)}, u32[]{:S(2)}) copy-start(bf16[1024,768]{1,0:T(8,128)(2,1)} %param.19) | copy-start | bytes 4718596
  920.1 1.2 copy-start.3
Sparse Core Ops, SparseCore 0:
  458.7 386.0 all-reduce.3
where the time goes:
time: 951 us; the launch traced here: 938 us
  waiting for transfers between devices  439 us (46%)
  local copies, waits for them, and re-layouts  369 us (39%)
  other arithmetic  46.6 us (5%)
  blocking collectives  35.7 us (4%)
  matrix products  17.9 us (2%)
  between operations  15 us (2%)
  starting transfers between devices  12 us (1%)
    unnamed x2, waiting for transfers between devices  266 us
    all_to_all x1, waiting for transfers between devices, on_device(): lax.all_to_all(answers, 'gx', split_axis=0, concat_axis=0, tiled=True)  174 us
    gather x28, local copies, waits for them, and re-layouts, segment_ids(): return jnp.searchsorted(ends, positions, side='right')  148 us
    gather x3, local copies, waits for them, and re-layouts, on_device(): answers = features[incoming]  53.7 us
    gather x12, local copies, waits for them, and re-layouts, on_device(): jnp.searchsorted(sorted_own, jnp.arange(devices, dtype=jnp.int32), side='...  37.7 us
    scatter-add x1, other arithmetic, forward_pass(): jax.ops.segment_sum(fetched[nodes:].astype(jnp.float32), hop2_ids, num_se...  21.3 us
    gather x1, local copies, waits for them, and re-layouts, on_device(): rank_sorted = jnp.arange(requests, dtype=jnp.int32) - first_pos[sorted_own]  19.5 us
    gather x1, local copies, waits for them, and re-layouts, on_device(): fetched = returned.reshape(devices * capacity, features.shape[1])[slot_of]  19.4 us
  transfers between devices with their start and end apart: 3, of which 2 were waited for; matrix products, arithmetic and copies ran while one was open for 18% of the time, Pallas kernels for 0%

commit v1 on v0

v1 whole, which is shorter than its diff:
```python
import jax
import jax.numpy as jnp
from jax import lax
from jax.experimental import pallas as pl
from jax.experimental.pallas import tpu as pltpu
from jax.sharding import PartitionSpec as P

BLOCK_ROWS = 128
DEVICES = 512
CAP = 12
LANES_CAP = 16
FIRST = 8
BOTH = ("gx", "gy")
F32 = jnp.float32
BF16 = jnp.bfloat16
MIB = 1 << 20


def iota(shape, dim):
    return lax.broadcasted_iota(jnp.int32, shape, dim)


def dot(a, b, dims=((1,), (0,))):
    return lax.dot_general(a, b, (dims, ((), ())), preferred_element_type=F32)


def params(mib, semantics=("arbitrary",)):
    return pltpu.CompilerParams(dimension_semantics=semantics, vmem_limit_bytes=mib * MIB)


def route_kernel(owner_ref, block_ref, offset_ref, hop2_ref, want_ref, node_ref):
    nodes = hop2_ref.shape[1]
    step = 256
    counts = hop2_ref[...].astype(F32)
    ends = jnp.sum(
        jnp.where(iota((nodes, nodes), 1) <= iota((nodes, nodes), 0), counts, 0.0),
        axis=1,
        keepdims=True,
    )
    before = (iota((step, step), 0) < iota((step, step), 1)).astype(BF16)
    owner_at = iota((DEVICES, step), 0)
    slot_at = iota((LANES_CAP, step), 0)
    carry = jnp.zeros((DEVICES, 1), F32)
    total = jnp.zeros((DEVICES, 2 * LANES_CAP), F32)
    for blk in range(owner_ref.shape[1] // step):
        at = pl.ds(blk * step, step)
        place = blk * step + iota((1, step), 1)
        if blk * step < nodes:
            node = place
        else:
            inside = (place - nodes).astype(F32)
            node = jnp.sum(jnp.where(ends <= inside, 1.0, 0.0), axis=0, keepdims=True).astype(
                jnp.int32
            )
        want = block_ref[:, at] * BLOCK_ROWS + offset_ref[:, at]
        here = owner_at == owner_ref[:, at]
        here_f = jnp.where(here, 1.0, 0.0)
        here_b = here_f.astype(BF16)
        seen = dot(here_b, before) + carry
        rank = jnp.sum(jnp.where(here, seen, 0.0), axis=0, keepdims=True).astype(jnp.int32)
        carry = carry + jnp.sum(here_f, axis=1, keepdims=True)
        mine = slot_at == rank

        def fields(part):
            return jnp.concatenate(
                [
                    jnp.where(mine, part(want + 1).astype(F32), 0.0),
                    jnp.where(mine, part(node + 1).astype(F32), 0.0),
                ],
                axis=0,
            ).astype(BF16)

        total = total + dot(here_b, fields(lambda v: v & ~31), ((1,), (1,)))
        total = total + dot(here_b, fields(lambda v: v & 31), ((1,), (1,)))
    total = total.astype(jnp.int32)
    want_ref[...] = total[:, :LANES_CAP]
    node_ref[...] = total[:, LANES_CAP:]


def route(owners, blocks, offsets, hop2):
    shape = jax.ShapeDtypeStruct((DEVICES, LANES_CAP), jnp.int32)
    return pl.pallas_call(
        route_kernel,
        out_shape=(shape, shape),
        compiler_params=pltpu.CompilerParams(vmem_limit_bytes=32 * MIB),
        cost_estimate=pl.CostEstimate(flops=4_000_000_000, bytes_accessed=200_000, transcendentals=0),
        name="route",
    )(owners, blocks, offsets, hop2)


def gather_kernel(folded, want_ref, features_ref, out_ref):
    readers, lanes = want_ref.shape
    rows = readers * 8
    spread = jnp.broadcast_to(want_ref[...].astype(F32)[:, None, :], (readers, 8, lanes))
    sub = iota((readers, 8, lanes), 1)
    slot = FIRST + (sub & 3) if folded else sub
    chosen = jnp.sum(
        jnp.where(iota((readers, 8, lanes), 2) == slot, spread, 0.0), axis=2, keepdims=True
    )
    chosen = chosen.reshape(rows, 1).astype(jnp.int32) - 1
    held = features_ref.shape[0]
    picks = jnp.where(iota((rows, held), 1) == chosen, 1.0, 0.0).astype(BF16)
    found = dot(picks, features_ref[...])
    if folded:
        half = found.shape[1] // 2
        low = (iota((rows, half), 0) & 7) < 4
        found = jnp.where(low, found[:, :half], found[:, half:])
    out_ref[...] = found.astype(BF16)


def gather(folded, want, features):
    width = features.shape[1] // 2 if folded else features.shape[1]
    readers = 64
    return pl.pallas_call(
        lambda *refs: gather_kernel(folded, *refs),
        grid=(DEVICES // readers,),
        in_specs=[
            pl.BlockSpec((readers, LANES_CAP), lambda i: (i, 0)),
            pl.BlockSpec(features.shape, lambda i: (0, 0)),
        ],
        out_specs=pl.BlockSpec((readers * 8, width), lambda i: (i, 0)),
        out_shape=jax.ShapeDtypeStruct((DEVICES * 8, width), BF16),
        compiler_params=params(48),
        cost_estimate=pl.CostEstimate(
            flops=2 * DEVICES * 8 * features.shape[0] * features.shape[1],
            bytes_accessed=DEVICES * 16 * width,
            transcendentals=0,
        ),
        name="gather_rest" if folded else "gather_first",
    )(want, features)


def sum_first_kernel(node_ref, rows_ref, out_ref):
    nodes, step = out_ref.shape[0], rows_ref.shape[0]
    takes = jnp.where(iota((nodes, step), 0) == node_ref[...] - 1, 1.0, 0.0).astype(BF16)
    part = dot(takes, rows_ref[...])

    @pl.when(pl.program_id(0) == 0)
    def _():
        out_ref[...] = part

    @pl.when(pl.program_id(0) > 0)
    def _():
        out_ref[...] += part


def sum_first(node, rows, nodes):
    step = 512
    count, width = rows.shape
    return pl.pallas_call(
        sum_first_kernel,
        grid=(count // step,),
        in_specs=[
            pl.BlockSpec((1, step), lambda i: (0, i)),
            pl.BlockSpec((step, width), lambda i: (i, 0)),
        ],
        out_specs=pl.BlockSpec((nodes, width), lambda i: (0, 0)),
        out_shape=jax.ShapeDtypeStruct((nodes, width), F32),
        compiler_params=params(48),
        cost_estimate=pl.CostEstimate(
            flops=2 * nodes * count * width, bytes_accessed=count * width * 2, transcendentals=0
        ),
        name="sum_first",
    )(node, rows)


def seed_groups(counts, nodes):
    seeds = counts.shape[1]
    row, col = iota((seeds, seeds), 0), iota((seeds, seeds), 1)
    ends = jnp.sum(jnp.where(col <= row, counts, 0.0), axis=1, keepdims=True)
    own = jnp.sum(jnp.where(col == row, counts, 0.0), axis=1, keepdims=True)
    seed, node = iota((seeds, nodes), 0), iota((seeds, nodes), 1)
    inside = (node - seeds).astype(F32)
    grouped = (node >= seeds) & (inside >= ends - own) & (inside < ends)
    return jnp.where(grouped | (seed == node), 1.0, 0.0).astype(BF16), 1.0 + own


def forward_kernel(node_ref, rows_ref, sums_ref, hop1_ref, hop2_ref, w1_ref, w2_ref, out_ref, acc_ref):
    nodes, step = sums_ref.shape[0], rows_ref.shape[0]
    half = rows_ref.shape[1]

    @pl.when(pl.program_id(0) == 0)
    def _():
        acc_ref[...] = sums_ref[...]

    takes = iota((nodes, step), 0) == node_ref[...] - 1
    low = (iota((nodes, step), 1) & 7) < 4
    acc_ref[:, :half] += dot(jnp.where(takes & low, 1.0, 0.0).astype(BF16), rows_ref[...])
    acc_ref[:, half:] += dot(
        jnp.where(takes & jnp.logical_not(low), 1.0, 0.0).astype(BF16), rows_ref[...]
    )

    @pl.when(pl.program_id(0) == pl.num_programs(0) - 1)
    def _():
        same = iota((nodes, nodes), 0) == iota((nodes, nodes), 1)
        counts = jnp.sum(
            jnp.where(same, hop2_ref[...].astype(F32), 0.0), axis=1, keepdims=True
        )
        agg_one = (acc_ref[...] / (1.0 + counts)).astype(BF16)
        groups, sizes = seed_groups(hop1_ref[...].astype(F32), nodes)
        scale = 1.0 / sizes
        total = jnp.zeros(out_ref.shape, F32)
        hid = w1_ref.shape[1]
        for at in range(0, hid, 256):
            pre = dot(agg_one, w1_ref[:, at : at + 256])
            hidden = (pre * jax.nn.sigmoid(pre)).astype(BF16)
            agg_two = (dot(groups, hidden) * scale).astype(BF16)
            total = total + dot(agg_two, w2_ref[at : at + 256, :])
        out_ref[...] = total


def forward(node, rows, sums, hop1, hop2, w1, w2):
    step = 512
    count, half = rows.shape
    nodes, width = sums.shape
    seeds, classes = hop1.shape[1], w2.shape[1]
    whole = lambda a: pl.BlockSpec(a.shape, lambda i: (0, 0))
    return pl.pallas_call(
        forward_kernel,
        grid=(count // step,),
        in_specs=[
            pl.BlockSpec((1, step), lambda i: (0, i)),
            pl.BlockSpec((step, half), lambda i: (i, 0)),
            whole(sums),
            whole(hop1),
            whole(hop2),
            whole(w1),
            whole(w2),
        ],
        out_specs=pl.BlockSpec((seeds, classes), lambda i: (0, 0)),
        out_shape=jax.ShapeDtypeStruct((seeds, classes), F32),
        scratch_shapes=[pltpu.VMEM((nodes, width), F32)],
        compiler_params=params(56),
        cost_estimate=pl.CostEstimate(
            flops=2 * nodes * count * width + 2 * nodes * width * w1.shape[1],
            bytes_accessed=count * half * 2,
            transcendentals=nodes * w1.shape[1],
        ),
        name="forward",
    )(node, rows, sums, hop1, hop2, w1, w2)


def backward_kernel(agg_ref, hop1_ref, cot_ref, w1_ref, w2_ref, hidden_ref, class_ref):
    nodes = agg_ref.shape[0]
    seeds = hop1_ref.shape[1]
    counts = hop1_ref[...].astype(F32)
    groups, sizes = seed_groups(counts, nodes)
    scale = 1.0 / sizes
    row, col = iota((seeds, seeds), 0), iota((seeds, seeds), 1)
    own = sizes - 1.0
    ends = jnp.sum(jnp.where(row <= col, own, 0.0), axis=0, keepdims=True)
    node, seed = iota((nodes, seeds), 0), iota((nodes, seeds), 1)
    inside = (node - seeds).astype(F32)
    grouped = (node >= seeds) & (inside >= ends - counts) & (inside < ends)
    hands = grouped | (seed == node)
    node_scale = jnp.sum(jnp.where(hands, 1.0 / (1.0 + counts), 0.0), axis=1, keepdims=True)
    cot = cot_ref[...]
    node_cot = dot(jnp.where(hands, 1.0, 0.0).astype(BF16), cot).astype(BF16)

    agg = agg_ref[...]
    pre = dot(agg, w1_ref[...])
    sigma = jax.nn.sigmoid(pre)
    hidden = (pre * sigma).astype(BF16)
    agg_two = (dot(groups, hidden) * scale).astype(BF16)
    class_ref[...] = dot(agg_two, cot, ((0,), (0,)))
    d_hidden = dot(node_cot, w2_ref[...], ((1,), (1,))) * node_scale
    d_pre = (d_hidden * sigma * (1.0 + pre * (1.0 - sigma))).astype(BF16)
    hidden_ref[...] = dot(d_pre, agg, ((0,), (0,)))


def backward(agg, hop1, cot, w1, w2):
    nodes, feat = agg.shape
    hid = w1.shape[1]
    seeds, classes = cot.shape
    step = 256
    whole = lambda a: pl.BlockSpec(a.shape, lambda i: (0, 0))
    return pl.pallas_call(
        backward_kernel,
        grid=(hid // step,),
        in_specs=[
            whole(agg),
            whole(hop1),
            whole(cot),
            pl.BlockSpec((feat, step), lambda i: (0, i)),
            pl.BlockSpec((step, classes), lambda i: (i, 0)),
        ],
        out_specs=(
            pl.BlockSpec((step, feat), lambda i: (i, 0)),
            pl.BlockSpec((step, classes), lambda i: (i, 0)),
        ),
        out_shape=(
            jax.ShapeDtypeStruct((hid, feat), F32),
            jax.ShapeDtypeStruct((hid, classes), F32),
        ),
        compiler_params=params(56),
        cost_estimate=pl.CostEstimate(
            flops=4 * nodes * feat * hid, bytes_accessed=6 * MIB, transcendentals=nodes * hid
        ),
        name="backward",
    )(agg, hop1, cot, w1, w2)


def exchange(rows):
    return lax.all_to_all(rows, BOTH, split_axis=0, concat_axis=0, tiled=True)


def on_device(
    features,
    hidden_weight,
    class_weight,
    req_owner,
    req_block,
    req_offset,
    hop1_counts,
    hop2_counts,
    prior_agg,
    prior_hop1,
    cotangent,
):
    outer, inner = lax.axis_size("gx"), lax.axis_size("gy")
    want, node = route(req_owner.reshape(1, -1), req_block, req_offset, hop2_counts)
    asked = lax.all_to_all(
        lax.all_to_all(
            want.reshape(outer, inner, LANES_CAP), "gx", split_axis=0, concat_axis=0, tiled=True
        ),
        "gy",
        split_axis=1,
        concat_axis=1,
        tiled=True,
    ).reshape(DEVICES, LANES_CAP)
    first = exchange(gather(False, asked, features))
    rest = exchange(gather(True, asked, features))

    hidden_term, class_term = backward(
        prior_agg, prior_hop1, cotangent, hidden_weight, class_weight
    )
    hidden_grad = lax.psum_scatter(hidden_term, "gx", scatter_dimension=0, tiled=True)
    hidden_grad = lax.psum_scatter(hidden_grad, "gy", scatter_dimension=0, tiled=True).T
    class_grad = lax.psum(class_term, BOTH)

    nodes = hop2_counts.shape[1]
    node_first = node[:, :FIRST].reshape(1, -1)
    tail = node[:, FIRST:CAP]
    node_rest = jnp.concatenate([tail, tail], axis=1).reshape(1, -1)
    sums = sum_first(node_first, first, nodes)
    logits = forward(
        node_rest, rest, sums, hop1_counts, hop2_counts, hidden_weight, class_weight
    )
    return (logits, hidden_grad, class_grad)


def solution(mesh):
    placed = (
        P(BOTH, None),
        P(),
        P(),
        P(BOTH, None, None),
        P(BOTH, None),
        P(BOTH, None),
        P(BOTH, None),
        P(BOTH, None),
        P(BOTH, None),
        P(BOTH, None),
        P(BOTH, None),
    )
    return jax.shard_map(
        on_device,
        mesh=mesh,
        in_specs=placed,
        out_specs=(P(BOTH, None), P(None, BOTH), P()),
        check_vma=False,
    )
```

time: 951 us -> 750 us (0.79); the launches traced: 938 us -> 749 us
  local copies, waits for them, and re-layouts: 369 us -> 17.5 us
  waiting for transfers between devices: 439 us -> 593 us
  Pallas kernels: 0 us -> 58.5 us
  other arithmetic: 46.6 us -> 2.61 us
  matrix products: 17.9 us -> 0 us
  starting transfers between devices: 12 us -> 24.9 us
    gather x47 -> x0, local copies, waits for them, and re-layouts: 299 us -> none  [the longest x28 148 us: segment_ids(): return jnp.searchsorted(ends, positions, side='right')]
    psum x0 -> x1, waiting for transfers between devices: none -> 233 us  [on_device(): class_grad = lax.psum(class_term, BOTH)]
    unnamed x2 -> x4, waiting for transfers between devices: 266 us -> 152 us
    reduce_scatter x0 -> x1, waiting for transfers between devices: none -> 86.6 us  [on_device(): lax.psum_scatter(hidden_term, 'gx', scatter_dimension=0, tiled=True)]
    pallas_call x0 -> x6, Pallas kernels: none -> 58.5 us  [the longest x2 19 us: gather(): pl.pallas_call(lambda *refs: gather_kernel(folded, *refs), grid=(DEVICES...]
    all_to_all x2, waiting for transfers between devices: 174 us -> 122 us  [exchange(): return lax.all_to_all(rows, BOTH, split_axis=0, concat_axis=0, tiled=True)]
    scatter-add x3 -> x0, other arithmetic: 32.6 us -> none  [the longest x1 21.3 us: forward_pass(): jax.ops.segment_sum(fetched[nodes:].astype(jnp.float32), hop2_ids, num_se...]
    scatter x2 -> x0, local copies, waits for them, and re-layouts: 23.6 us -> none  [the longest x1 11.8 us: on_device(): outgoing = jnp.zeros((devices * capacity,), jnp.int32).at[slot_of].set(wa...]
  transfers between devices with their start and end apart: 3 -> 5, of which waited for: 2 -> 4; matrix products, arithmetic and copies ran while one was open for 18% -> 1% of each run, Pallas kernels for 0% -> 4%
where the time goes in v1:
time: 750 us; the launch traced here: 749 us
  waiting for transfers between devices  593 us (79%)
  Pallas kernels  58.5 us (8%)
  blocking collectives  35.7 us (5%)
  starting transfers between devices  24.9 us (3%)
  local copies, waits for them, and re-layouts  17.5 us (2%)
  between operations  16.3 us (2%)
    psum x1, waiting for transfers between devices, on_device(): class_grad = lax.psum(class_term, BOTH)  233 us
    unnamed x4, waiting for transfers between devices  152 us
    all_to_all x2, waiting for transfers between devices, exchange(): return lax.all_to_all(rows, BOTH, split_axis=0, concat_axis=0, tiled=True)  122 us
    reduce_scatter x1, waiting for transfers between devices, on_device(): lax.psum_scatter(hidden_term, 'gx', scatter_dimension=0, tiled=True)  86.6 us
    all_to_all x2, starting transfers between devices, exchange(): return lax.all_to_all(rows, BOTH, split_axis=0, concat_axis=0, tiled=True)  24.6 us
    pallas_call x2, Pallas kernels, gather(): pl.pallas_call(lambda *refs: gather_kernel(folded, *refs), grid=(DEVICES...  19 us
    all_to_all x1, blocking collectives, on_device(): lax.all_to_all(want.reshape(outer, inner, LANES_CAP), 'gx', split_axis=0,...  17.9 us
    all_to_all x1, blocking collectives, on_device(): lax.all_to_all(lax.all_to_all(want.reshape(outer, inner, LANES_CAP), 'gx'...  17.8 us
  transfers between devices with their start and end apart: 5, of which 4 were waited for; matrix products, arithmetic and copies ran while one was open for 1% of the time, Pallas kernels for 4%

profile of v1, /device:TPU:16, one launch (start us, length us, event | category | flops | bytes accessed | tf_op | source)
XLA Modules:
  0.0 748.6 jit_solution(16288785333660032107)
XLA Ops:
  10.8 5.3 route.1
  16.4 17.9 %all_to_all.32 = s32[16,1,512]{2,1,0:T(1,128)S(1)} all-to-all(s32[16,1,512]{2,1,0:T(1,128)S(1)} %reshape.31), channel_id=1, replica_groups=mesh['gx'=16,'gy'=32] {'gx'}, dimensions={0} | all-to-all | bytes 65536 | tf_op jit(solution)/shard_map/all_to_all | solution.py:323
  35.9 17.8 %all_to_all.33 = s32[32,1,256]{2,1,0:T(1,128)S(1)} all-to-all(s32[32,1,256]{2,1,0:T(1,128)S(1)} %reshape.33), channel_id=1, replica_groups=mesh['gx'=16,'gy'=32] {'gy'}, dimensions={0} | all-to-all | bytes 65536 | tf_op jit(solution)/shard_map/all_to_all | solution.py:322
  54.7 9.6 %gather_first.1 = bf16[4096,768]{1,0:T(8,128)(2,1)} custom-call(s32[512,16]{1,0:T(8,128)S(1)} %bitcast.17, bf16[1024,768]{1,0:T(8,128)(2,1)S(1)} %copy-done), custom_call_target="tpu_custom_call" | custom-call | flops 6442450944 | bytes 6291456 | tf_op jit(solution)/shard_map/gather_first/pallas_call | solution.py:114
  64.3 13.1 %all-to-all-start.3 = ((bf16[512,8,768]{2,1,0:T(8,128)(2,1)}), bf16[512,8,768]{2,1,0:T(8,128)(2,1)}, u32[]{:S(2)}, u32[]{:S(2)}) async-start(bf16[512,8,768]{2,1,0:T(8,128)(2,1)} %bitcast.20), calls=%async_computation.3 | async-start | bytes 12582912 | tf_op jit(solution)/shard_map/all_to_all | solution.py:304
  77.6 1.0 copy.38.w2_ref
  79.4 9.9 %backward.1 = (f32[1024,768]{1,0:T(8,128)}, f32[1024,153]{1,0:T(8,128)}) custom-call(bf16[768,768]{1,0:T(8,128)(2,1)} %agg_ref.1, s32[1,256]{1,0:T(1,128)} %hop1_ref.3, bf16[256,153]{1,0:T(8,128)(2,1)} %copy.39.cot_ref, bf16[768,1024]{1,0:T(8,128)(2,1)} %w1_ref.3, bf16[1024,153]{1,0:T(8,128)(2,1)} %copy.38.w2_ref), custom_call_target="tpu_custom_call" | custom-call | flops 2415919104 | bytes 6291456 | tf_op jit(solution)/shard_map/backward/pallas_call | solution.py:277
  89.3 9.4 %gather_rest.1 = bf16[4096,384]{1,0:T(8,128)(2,1)} custom-call(s32[512,16]{1,0:T(8,128)S(1)} %bitcast.18, bf16[1024,768]{1,0:T(8,128)(2,1)S(1)} %copy-done), custom_call_target="tpu_custom_call" | custom-call | flops 6442450944 | bytes 3145728 | tf_op jit(solution)/shard_map/gather_rest/pallas_call | solution.py:114
  98.8 121.7 %all-to-all-done.3 = bf16[512,8,768]{2,1,0:T(8,128)(2,1)} async-done(((bf16[512,8,768]{2,1,0:T(8,128)(2,1)}), bf16[512,8,768]{2,1,0:T(8,128)(2,1)}, u32[]{:S(2)}, u32[]{:S(2)}) %all-to-all-start.3) | async-done | bytes 6291488 | tf_op jit(solution)/shard_map/all_to_all | solution.py:304
  220.4 11.5 %all-to-all-start.2 = ((bf16[512,8,384]{2,1,0:T(8,128)(2,1)}), bf16[512,8,384]{2,1,0:T(8,128)(2,1)S(1)}, u32[]{:S(2)}, u32[]{:S(2)}) async-start(bf16[512,8,384]{2,1,0:T(8,128)(2,1)} %bitcast.3), calls=%async_computation.2 | async-start | bytes 6291456 | tf_op jit(solution)/shard_map/all_to_all | solution.py:304
  232.5 86.6 %reduce-scatter.2.cloned.1.call-done = f32[64,768]{1,0:T(8,128)} async-done(((f32[1024,768]{1,0:T(8,128)}), f32[64,768]{1,0:T(8,128)}) %reduce-scatter.2.cloned.1.call-update) | async-done | bytes 196624 | tf_op jit(solution)/shard_map/reduce_scatter | solution.py:337
  319.1 0.8 slice.6
  320.2 1.2 pad_add_fusion
  321.3 0.8 reshape.26.node_ref
  322.1 1.3 dynamic-slice
  324.0 233.0 %all-reduce.4.cloned.1.call-done = f32[1024,153]{1,0:T(8,128)} async-done(((f32[1024,153]{1,0:T(8,128)}), f32[1024,153]{1,0:T(8,128)}) %all-reduce.4.cloned.1.call-update) | async-done | bytes 626704 | tf_op jit(solution)/shard_map/psum | solution.py:339
  557.1 2.4 copy.42
  559.4 151.2 %all-reduce.6.cloned.1.call-done = f32[64,768]{1,0:T(8,128)} async-done(((f32[64,768]{1,0:T(8,128)}), f32[64,768]{1,0:T(8,128)}) %all-reduce.6.cloned.1.call-update) | async-done | bytes 196624
  710.7 1.3 dynamic-slice_bitcast_fusion
  712.0 9.6 %sum_first.1.sums_ref = f32[768,768]{1,0:T(8,128)S(1)} custom-call(s32[1,4096]{1,0:T(1,128)S(1)} %reshape.29.node_ref, bf16[4096,768]{1,0:T(8,128)(2,1)} %bitcast.6.rows_ref), custom_call_target="tpu_custom_call" | custom-call | flops 4831838208 | bytes 6291456 | tf_op jit(solution)/shard_map/sum_first/pallas_call | solution.py:150
  721.6 1.5 copy-done.5
  723.1 1.6 copy-done.6
  724.7 14.7 %forward.1 = f32[256,153]{1,0:T(8,128)} custom-call(s32[1,4096]{1,0:T(1,128)} %reshape.26.node_ref, bf16[4096,384]{1,0:T(8,128)(2,1)} %bitcast.21, f32[768,768]{1,0:T(8,128)} %copy-done.5, s32[1,256]{1,0:T(1,128)} %hop1_ref.2, s32[1,768]{1,0:T(1,128)} %hop2_ref.3, bf16[768,1024]{1,0:T(8,128)(2,1)} %w1_ref.3, bf16[1024,153]{1,0:T(8,128)(2,1)} %copy.38.w2_ref), custom_call_target="tpu_custom_call" | custom-call | flops 6039797760 | bytes 3145728 | tf_op jit(solution)/shard_map/forward/pallas_call | solution.py:218
  739.4 1.7 copy.41
  (35 shorter events, 7.4 us)
Async XLA Ops:
  8.0 0.7 copy-start.1
  8.7 0.7 copy-start.2
  9.4 0.7 copy-start.3
  10.1 0.7 copy-start.4
  10.8 43.9 %copy-start = (bf16[1024,768]{1,0:T(8,128)(2,1)S(1)}, bf16[1024,768]{1,0:T(8,128)(2,1)}, u32[]{:S(2)}) copy-start(bf16[1024,768]{1,0:T(8,128)(2,1)} %refs_1_.3) | copy-start | bytes 4718596
  64.3 13.3 %copy-start.7 = (bf16[1024,153]{0,1:T(8,128)(2,1)S(1)}, bf16[1024,153]{0,1:T(8,128)(2,1)}, u32[]{:S(2)}) copy-start(bf16[1024,153]{0,1:T(8,128)(2,1)} %param.13) | copy-start | bytes 940036
  64.3 14.3 %copy-start.8 = (bf16[256,153]{0,1:T(8,128)(2,1)S(1)}, bf16[256,153]{0,1:T(8,128)(2,1)}, u32[]{:S(2)}) copy-start(bf16[256,153]{0,1:T(8,128)(2,1)} %param.21) | copy-start | bytes 235012
  64.3 156.1 %all-to-all-start.3 = ((bf16[512,8,768]{2,1,0:T(8,128)(2,1)}), bf16[512,8,768]{2,1,0:T(8,128)(2,1)}, u32[]{:S(2)}, u32[]{:S(2)}) async-start(bf16[512,8,768]{2,1,0:T(8,128)(2,1)} %bitcast.20), calls=%async_computation.3 | async-start | bytes 12582912 | tf_op jit(solution)/shard_map/all_to_all | solution.py:304
  77.4 241.7 %reduce-scatter.2.cloned.1.call-start = ((), (), s32[]{:S(2)}) async-start(), calls=%async_computation.5 | async-start | bytes 3342336 | tf_op jit(solution)/shard_map/reduce_scatter | solution.py:337
  220.4 502.7 %all-to-all-start.2 = ((bf16[512,8,384]{2,1,0:T(8,128)(2,1)}), bf16[512,8,384]{2,1,0:T(8,128)(2,1)S(1)}, u32[]{:S(2)}, u32[]{:S(2)}) async-start(bf16[512,8,384]{2,1,0:T(8,128)(2,1)} %bitcast.3), calls=%async_computation.2 | async-start | bytes 6291456 | tf_op jit(solution)/shard_map/all_to_all | solution.py:304
  231.9 325.1 %all-reduce.4.cloned.1.call-start = ((), (), s32[]{:S(2)}) async-start(), calls=%async_computation.6 | async-start | bytes 2097152 | tf_op jit(solution)/shard_map/psum | solution.py:339
  232.5 478.2 %all-reduce.6.cloned.1.call-start = ((), (), s32[]{:S(2)}) async-start(), calls=%async_computation.7 | async-start | bytes 393216
  721.6 1.5 copy-start.5
  723.1 1.6 copy-start.6
Sparse Core Ops, SparseCore 0:
  89.5 229.6 reduce-scatter.1
Sparse Core Ops, SparseCore 1:
  237.5 319.5 all-reduce.3
  560.7 149.9 all-reduce.5

commit v2 on v1

v2 whole, which is shorter than its diff:
```python
import jax
import jax.numpy as jnp
from jax import lax
from jax.experimental import pallas as pl
from jax.experimental.pallas import tpu as pltpu
from jax.sharding import PartitionSpec as P

BLOCK_ROWS = 128
DEVICES = 512
CAP = 12
LANES_CAP = 16
FIRST = 8
PIECE = 128
BOTH = ("gx", "gy")
Z, CORES, X, Y = 8, 2, 4, 8
F32 = jnp.float32
BF16 = jnp.bfloat16
MIB = 1 << 20


def iota(shape, dim):
    return lax.broadcasted_iota(jnp.int32, shape, dim)


def dot(a, b, dims=((1,), (0,))):
    return lax.dot_general(a, b, (dims, ((), ())), preferred_element_type=F32)


def params(mib, semantics=("arbitrary",)):
    return pltpu.CompilerParams(dimension_semantics=semantics, vmem_limit_bytes=mib * MIB)


def route_kernel(owner_ref, block_ref, offset_ref, hop2_ref, want_ref, node_ref):
    nodes = hop2_ref.shape[1]
    step = 256
    counts = hop2_ref[...].astype(F32)
    ends = jnp.sum(
        jnp.where(iota((nodes, nodes), 1) <= iota((nodes, nodes), 0), counts, 0.0),
        axis=1,
        keepdims=True,
    )
    before = (iota((step, step), 0) < iota((step, step), 1)).astype(BF16)
    owner_at = iota((DEVICES, step), 0)
    slot_at = iota((LANES_CAP, step), 0)
    carry = jnp.zeros((DEVICES, 1), F32)
    total = jnp.zeros((DEVICES, 2 * LANES_CAP), F32)
    for blk in range(owner_ref.shape[1] // step):
        at = pl.ds(blk * step, step)
        place = blk * step + iota((1, step), 1)
        if blk * step < nodes:
            node = place
        else:
            inside = (place - nodes).astype(F32)
            node = jnp.sum(jnp.where(ends <= inside, 1.0, 0.0), axis=0, keepdims=True).astype(
                jnp.int32
            )
        want = block_ref[:, at] * BLOCK_ROWS + offset_ref[:, at]
        here = owner_at == owner_ref[:, at]
        here_f = jnp.where(here, 1.0, 0.0)
        here_b = here_f.astype(BF16)
        seen = dot(here_b, before) + carry
        rank = jnp.sum(jnp.where(here, seen, 0.0), axis=0, keepdims=True).astype(jnp.int32)
        carry = carry + jnp.sum(here_f, axis=1, keepdims=True)
        mine = slot_at == rank

        def fields(part):
            return jnp.concatenate(
                [
                    jnp.where(mine, part(want + 1).astype(F32), 0.0),
                    jnp.where(mine, part(node + 1).astype(F32), 0.0),
                ],
                axis=0,
            ).astype(BF16)

        total = total + dot(here_b, fields(lambda v: v & ~31), ((1,), (1,)))
        total = total + dot(here_b, fields(lambda v: v & 31), ((1,), (1,)))
    total = total.astype(jnp.int32)
    want_ref[...] = total[:, :LANES_CAP]
    node_ref[...] = total[:, LANES_CAP:]


def route(owners, blocks, offsets, hop2):
    shape = jax.ShapeDtypeStruct((DEVICES, LANES_CAP), jnp.int32)
    return pl.pallas_call(
        route_kernel,
        out_shape=(shape, shape),
        compiler_params=pltpu.CompilerParams(vmem_limit_bytes=32 * MIB),
        cost_estimate=pl.CostEstimate(flops=4_000_000_000, bytes_accessed=200_000, transcendentals=0),
        name="route",
    )(owners, blocks, offsets, hop2)


def picks_of(want_ref, held, slot_of):
    readers, lanes = want_ref.shape
    rows = readers * 8
    spread = jnp.broadcast_to(want_ref[...].astype(F32)[:, None, :], (readers, 8, lanes))
    slot = slot_of(iota((readers, 8, lanes), 1))
    chosen = jnp.sum(
        jnp.where(iota((readers, 8, lanes), 2) == slot, spread, 0.0), axis=2, keepdims=True
    )
    chosen = chosen.reshape(rows, 1).astype(jnp.int32) - 1
    return jnp.where(iota((rows, held), 1) == chosen, 1.0, 0.0).astype(BF16)


def gather_kernel(part, want_ref, features_ref, after_ref, out_ref):
    held = features_ref.shape[0]
    if part == 1:
        found = dot(picks_of(want_ref, held, lambda sub: FIRST + (sub & 3)), features_ref[...])
        half = found.shape[1] // 2
        low = (iota((found.shape[0], half), 0) & 7) < 4
        out_ref[...] = jnp.where(low, found[:, :half], found[:, half:]).astype(BF16)
        return
    half = features_ref.shape[1]
    found = dot(picks_of(want_ref, held, lambda sub: sub), features_ref[...])
    out_ref[:, :half] = found.astype(BF16)
    if part == 2:
        last = dot(
            picks_of(want_ref, held, lambda sub: jnp.where(sub < 2, CAP - 2 + sub, LANES_CAP)),
            features_ref[:, half - PIECE :],
        )
        out_ref[:, half:] = last.astype(BF16)


def gather(part, want, features, after):
    held, width = features.shape
    half = width // 2
    sent = half + PIECE if part == 2 else half
    readers = 64
    if part == 1:
        source = pl.BlockSpec((held, width), lambda i: (0, 0))
    else:
        source = pl.BlockSpec((held, half), lambda i: (0, part // 2))
    return pl.pallas_call(
        lambda *refs: gather_kernel(part, *refs),
        grid=(DEVICES // readers,),
        in_specs=[
            pl.BlockSpec((readers, LANES_CAP), lambda i: (i, 0)),
            source,
            pl.BlockSpec(memory_space=pl.ANY),
        ],
        out_specs=pl.BlockSpec((readers * 8, sent), lambda i: (i, 0)),
        out_shape=jax.ShapeDtypeStruct((DEVICES * 8, sent), BF16),
        compiler_params=params(32),
        cost_estimate=pl.CostEstimate(
            flops=2 * DEVICES * 8 * held * (half if part == 0 else width),
            bytes_accessed=DEVICES * 16 * sent,
            transcendentals=0,
        ),
        name=f"gather_{part}",
    )(want, features, after)


def taken(node_ref, nodes):
    return iota((nodes, node_ref.shape[1]), 0) == node_ref[...] - 1


def zero_one(mask):
    return jnp.where(mask, 1.0, 0.0).astype(BF16)


def add_up(out_ref, part):
    @pl.when(pl.program_id(0) == 0)
    def _():
        out_ref[...] = part

    @pl.when(pl.program_id(0) > 0)
    def _():
        out_ref[...] += part


def whole(a):
    return pl.BlockSpec(a.shape, lambda i: (0,) * a.ndim)


def sum_slots_kernel(node_ref, rows_ref, out_ref):
    add_up(out_ref, dot(zero_one(taken(node_ref, out_ref.shape[0])), rows_ref[...]))


def sum_slots(node, rows, nodes):
    step = 1024
    count, half = rows.shape
    return pl.pallas_call(
        sum_slots_kernel,
        grid=(count // step,),
        in_specs=[
            pl.BlockSpec((1, step), lambda i: (0, i)),
            pl.BlockSpec((step, half), lambda i: (i, 0)),
        ],
        out_specs=pl.BlockSpec((nodes, half), lambda i: (0, 0)),
        out_shape=jax.ShapeDtypeStruct((nodes, half), F32),
        compiler_params=params(32),
        cost_estimate=pl.CostEstimate(
            flops=2 * nodes * count * half, bytes_accessed=count * half * 2, transcendentals=0
        ),
        name="sum_slots",
    )(node, rows)


def group_sizes(hop2_ref):
    nodes = hop2_ref.shape[1]
    same = iota((nodes, nodes), 0) == iota((nodes, nodes), 1)
    counts = jnp.where(same, hop2_ref[...].astype(F32), 0.0)
    return 1.0 + jnp.sum(counts, axis=1, keepdims=True)


def sum_folded_kernel(node_ref, rows_ref, sums_ref, hop2_ref, w1_ref, pre_ref, high_ref, low_ref):
    nodes, half = sums_ref.shape
    takes = taken(node_ref, nodes)
    low = (iota(takes.shape, 1) & 7) < 4
    rows = rows_ref[...]
    ride = rows[:, half - PIECE :].astype(F32)
    ride = jnp.where((iota(ride.shape, 0) & 7) >= 6, 0.0, ride).astype(BF16)
    rows = jnp.concatenate([rows[:, : half - PIECE], ride], axis=1)
    add_up(low_ref, dot(zero_one(takes & low), rows))
    add_up(high_ref, dot(zero_one(takes & jnp.logical_not(low)), rows))

    @pl.when(pl.program_id(0) == pl.num_programs(0) - 1)
    def _():
        agg = ((sums_ref[...] + low_ref[...]) / group_sizes(hop2_ref)).astype(BF16)
        pre_ref[...] = dot(agg, w1_ref[...])


def sum_folded(node, rows, sums, hop2, w1):
    step = 1024
    count, half = rows.shape
    nodes, hid = sums.shape[0], w1.shape[1]
    return pl.pallas_call(
        sum_folded_kernel,
        grid=(count // step,),
        in_specs=[
            pl.BlockSpec((1, step), lambda i: (0, i)),
            pl.BlockSpec((step, half), lambda i: (i, 0)),
            whole(sums),
            whole(hop2),
            pl.BlockSpec((half, hid), lambda i: (0, 0)),
        ],
        out_specs=(
            pl.BlockSpec((nodes, hid), lambda i: (0, 0)),
            pl.BlockSpec((nodes, half), lambda i: (0, 0)),
        ),
        out_shape=(
            jax.ShapeDtypeStruct((nodes, hid), F32),
            jax.ShapeDtypeStruct((nodes, half), F32),
        ),
        scratch_shapes=[pltpu.VMEM((nodes, half), F32)],
        compiler_params=params(48),
        cost_estimate=pl.CostEstimate(
            flops=4 * nodes * count * half, bytes_accessed=count * half * 2, transcendentals=0
        ),
        name="sum_folded",
    )(node, rows, sums, hop2, w1)


def seed_groups(counts, nodes):
    seeds = counts.shape[1]
    row, col = iota((seeds, seeds), 0), iota((seeds, seeds), 1)
    ends = jnp.sum(jnp.where(col <= row, counts, 0.0), axis=1, keepdims=True)
    own = jnp.sum(jnp.where(col == row, counts, 0.0), axis=1, keepdims=True)
    seed, node = iota((seeds, nodes), 0), iota((seeds, nodes), 1)
    inside = (node - seeds).astype(F32)
    grouped = (node >= seeds) & (inside >= ends - own) & (inside < ends)
    return jnp.where(grouped | (seed == node), 1.0, 0.0).astype(BF16), 1.0 + own


def forward_kernel(
    node_ref,
    last_ref,
    rows_ref,
    sums_ref,
    pre_ref,
    hop1_ref,
    hop2_ref,
    w1_ref,
    w2_ref,
    out_ref,
    acc_ref,
):
    nodes, half = sums_ref.shape
    add_up(acc_ref, dot(zero_one(taken(node_ref, nodes)), rows_ref[:, :half]))
    acc_ref[:, half - PIECE :] += dot(zero_one(taken(last_ref, nodes)), rows_ref[:, half:])

    @pl.when(pl.program_id(0) == pl.num_programs(0) - 1)
    def _():
        agg_one = ((sums_ref[...] + acc_ref[...]) / group_sizes(hop2_ref)).astype(BF16)
        groups, sizes = seed_groups(hop1_ref[...].astype(F32), nodes)
        scale = 1.0 / sizes
        total = jnp.zeros(out_ref.shape, F32)
        for at in range(0, w1_ref.shape[1], 256):
            pre = pre_ref[:, at : at + 256] + dot(agg_one, w1_ref[:, at : at + 256])
            hidden = (pre * jax.nn.sigmoid(pre)).astype(BF16)
            agg_two = (dot(groups, hidden) * scale).astype(BF16)
            total = total + dot(agg_two, w2_ref[at : at + 256, :])
        out_ref[...] = total


def forward(node, last, rows, sums, pre, hop1, hop2, w1, w2):
    step = 1024
    count, sent = rows.shape
    nodes, half = sums.shape
    hid = w1.shape[1]
    seeds, classes = hop1.shape[1], w2.shape[1]
    return pl.pallas_call(
        forward_kernel,
        grid=(count // step,),
        in_specs=[
            pl.BlockSpec((1, step), lambda i: (0, i)),
            pl.BlockSpec((1, step), lambda i: (0, i)),
            pl.BlockSpec((step, sent), lambda i: (i, 0)),
            whole(sums),
            whole(pre),
            whole(hop1),
            whole(hop2),
            pl.BlockSpec((half, hid), lambda i: (1, 0)),
            whole(w2),
        ],
        out_specs=pl.BlockSpec((seeds, classes), lambda i: (0, 0)),
        out_shape=jax.ShapeDtypeStruct((seeds, classes), F32),
        scratch_shapes=[pltpu.VMEM((nodes, half), F32)],
        compiler_params=params(48),
        cost_estimate=pl.CostEstimate(
            flops=2 * nodes * count * half + 2 * nodes * half * hid,
            bytes_accessed=count * half * 2,
            transcendentals=nodes * hid,
        ),
        name="forward",
    )(node, last, rows, sums, pre, hop1, hop2, w1, w2)


def backward_kernel(
    core_ref, agg_ref, hop1_ref, cot_ref, w1_ref, w2_ref, after_ref, kept_ref, sent_ref
):
    nodes = agg_ref.shape[0]
    seeds = hop1_ref.shape[1]
    counts = hop1_ref[...].astype(F32)
    groups, sizes = seed_groups(counts, nodes)
    scale = 1.0 / sizes
    row, col = iota((seeds, seeds), 0), iota((seeds, seeds), 1)
    own = sizes - 1.0
    ends = jnp.sum(jnp.where(row <= col, own, 0.0), axis=0, keepdims=True)
    node, seed = iota((nodes, seeds), 0), iota((nodes, seeds), 1)
    inside = (node - seeds).astype(F32)
    grouped = (node >= seeds) & (inside >= ends - counts) & (inside < ends)
    hands = grouped | (seed == node)
    node_scale = jnp.sum(jnp.where(hands, 1.0 / (1.0 + counts), 0.0), axis=1, keepdims=True)
    cot = cot_ref[...]
    node_cot = dot(jnp.where(hands, 1.0, 0.0).astype(BF16), cot).astype(BF16)

    agg = agg_ref[...]
    pre = dot(agg, w1_ref[...])
    sigma = jax.nn.sigmoid(pre)
    hidden = (pre * sigma).astype(BF16)
    agg_two = (dot(groups, hidden) * scale).astype(BF16)
    classes = cot.shape[1]
    wide = zero_one(iota((classes, 2 * PIECE), 0) == iota((classes, 2 * PIECE), 1))
    class_term = dot(agg_two, dot(cot, wide).astype(BF16), ((0,), (0,)))
    d_hidden = dot(node_cot, w2_ref[...], ((1,), (1,))) * node_scale
    d_pre = (d_hidden * sigma * (1.0 + pre * (1.0 - sigma))).astype(BF16)
    hidden_term = dot(d_pre, agg, ((0,), (0,)))
    first = core_ref[0] == 0
    half = kept_ref.shape[1] // 2
    mine = slice(0, half), slice(half, 2 * half)
    low = hidden_term[:, :half], hidden_term[:, half : 2 * half]
    high = hidden_term[:, 2 * half :], class_term
    for at, a, b in zip(mine, low, high):
        kept_ref[:, at] = jnp.where(first, a, b)
        sent_ref[:, at] = jnp.where(first, b, a)


def backward(core, agg, hop1, cot, w1, w2, after):
    nodes, feat = agg.shape
    hid = w1.shape[1]
    classes = cot.shape[1]
    step = 256
    half = (feat + 2 * PIECE) // 2
    return pl.pallas_call(
        backward_kernel,
        grid=(hid // step,),
        in_specs=[
            pl.BlockSpec(memory_space=pltpu.SMEM),
            whole(agg),
            whole(hop1),
            whole(cot),
            pl.BlockSpec((feat, step), lambda i: (0, i)),
            pl.BlockSpec((step, classes), lambda i: (i, 0)),
            pl.BlockSpec(memory_space=pl.ANY),
        ],
        out_specs=[pl.BlockSpec((step, half), lambda i: (i, 0))] * 2,
        out_shape=[jax.ShapeDtypeStruct((hid, half), F32)] * 2,
        compiler_params=params(48),
        cost_estimate=pl.CostEstimate(
            flops=4 * nodes * feat * hid, bytes_accessed=6 * MIB, transcendentals=nodes * hid
        ),
        name="backward",
    )(core, agg, hop1, cot, w1, w2, after)


def swap(rows, axis, bit):
    size = lax.axis_size(axis)
    return lax.ppermute(rows, axis, [(i, i ^ bit) for i in range(size)])


def split_kernel(x_ref, kept_ref, got_ref, own_ref, *sent_refs):
    def piece(k):
        at = pl.ds(pl.multiple_of(k * PIECE, PIECE), PIECE)
        return kept_ref[:, at] + got_ref[:, at]

    x = x_ref[0]
    own_ref[...] = piece(x)
    for k, ref in enumerate(sent_refs, 1):
        ref[...] = piece(x ^ k).astype(BF16)


def split(x, kept, got):
    rows, width = kept.shape
    step = 256
    block = pl.BlockSpec((step, width), lambda i: (i, 0))
    return pl.pallas_call(
        split_kernel,
        grid=(rows // step,),
        in_specs=[pl.BlockSpec(memory_space=pltpu.SMEM), block, block],
        out_specs=[pl.BlockSpec((step, PIECE), lambda i: (i, 0))] * X,
        out_shape=[jax.ShapeDtypeStruct((rows, PIECE), F32)]
        + [jax.ShapeDtypeStruct((rows, PIECE), BF16)] * (X - 1),
        compiler_params=params(16),
        name="split",
    )(x, kept, got)


def ride_sums_kernel(own_ref, *refs):
    got, rows_ref, out_ref = refs[: X - 1], refs[X - 1], refs[X]
    piece = own_ref[...]
    for ref in got:
        piece = piece + ref[...].astype(F32)
    shape = rows_ref.shape[0], piece.shape[0]
    i, j = iota(shape, 0), iota(shape, 1)
    put = dot(zero_one(((i >> 3) == (j >> 1)) & ((i & 7) == 6 + (j & 1))), piece.astype(BF16))
    ride = (iota(rows_ref.shape, 0) & 7) >= 6
    out_ref[...] = jnp.where(ride, put, rows_ref[...].astype(F32)).astype(BF16)


def ride_sums(own, got, rows):
    readers = 64
    mine = pl.BlockSpec((readers * 2, PIECE), lambda i: (i, 0))
    tile = pl.BlockSpec((readers * 8, PIECE), lambda i: (i, rows.shape[1] // PIECE - 1))
    return pl.pallas_call(
        ride_sums_kernel,
        grid=(DEVICES // readers,),
        in_specs=[mine] * X + [tile],
        out_specs=tile,
        out_shape=jax.ShapeDtypeStruct(rows.shape, BF16),
        input_output_aliases={X: 0},
        compiler_params=params(16),
        name="ride_sums",
    )(own, *got, rows)


def own_sums_kernel(rows_ref, out_ref, tile_ref):
    count = rows_ref.shape[0]
    shape = out_ref.shape[0], count
    j, i = iota(shape, 0), pl.program_id(0) * count + iota(shape, 1)
    add_up(out_ref, dot(zero_one((((i >> 6) & 7) == (j >> 1)) & ((i & 7) == 6 + (j & 1))), rows_ref[...]))

    @pl.when(pl.program_id(0) == pl.num_programs(0) - 1)
    def _():
        total = out_ref[...]
        high = total.astype(BF16).astype(F32)
        low = total - high
        tile_ref[...] = jnp.zeros(tile_ref.shape, F32)
        tile_ref[2:4, :] = high[12:14]
        tile_ref[4:6, :] = low[12:14]
        tile_ref[6:7, :] = (
            high[14:15]
            + pltpu.roll(high[15:16], 32, 1)
            + pltpu.roll(low[14:15], 64, 1)
            + pltpu.roll(low[15:16], 96, 1)
        )


def own_sums(rows):
    step = 2048
    return pl.pallas_call(
        own_sums_kernel,
        grid=(rows.shape[0] // step,),
        in_specs=[pl.BlockSpec((step, PIECE), lambda i: (i, rows.shape[1] // PIECE - 1))],
        out_specs=[
            pl.BlockSpec((16, PIECE), lambda i: (0, 0)),
            pl.BlockSpec((8, PIECE), lambda i: (0, 0)),
        ],
        out_shape=[
            jax.ShapeDtypeStruct((16, PIECE), F32),
            jax.ShapeDtypeStruct((8, PIECE), F32),
        ],
        compiler_params=params(16),
        name="own_sums",
    )(rows)


def ride_class_kernel(tile_ref, rows_ref, after_ref, out_ref):
    count = rows_ref.shape[0]
    tile = jnp.broadcast_to(tile_ref[...][None], (count // 8, 8, PIECE)).reshape(count, PIECE)
    ride = (iota(rows_ref.shape, 0) & 7) >= 2
    out_ref[...] = jnp.where(ride, tile, rows_ref[...].astype(F32)).astype(BF16)


def ride_class(tile, rows, after):
    step = 1024
    last = pl.BlockSpec((step, PIECE), lambda i: (i, rows.shape[1] // PIECE - 1))
    return pl.pallas_call(
        ride_class_kernel,
        grid=(rows.shape[0] // step,),
        in_specs=[whole(tile), last, pl.BlockSpec(memory_space=pl.ANY)],
        out_specs=last,
        out_shape=jax.ShapeDtypeStruct(rows.shape, BF16),
        input_output_aliases={1: 0},
        compiler_params=params(16),
        name="ride_class",
    )(tile, rows, after)


def class_rows_kernel(rows_ref, out_ref):
    rows = rows_ref[...]
    shape = out_ref.shape[0], rows.shape[0]
    j, i = iota(shape, 0), iota(shape, 1)
    sender, row, sub = (i >> 3) == (j >> 1), j & 1, i & 7
    first = dot(zero_one(sender & ((sub == 2 + row) | (sub == 4 + row))), rows)
    rest = dot(zero_one(sender & (sub == 6)), rows)
    rest = rest + pltpu.roll(rest, 64, 1)
    odd = (iota(rest.shape, 0) & 1) == 1
    rest = jnp.where(odd, pltpu.roll(rest, 96, 1), rest)
    out_ref[:, :PIECE] = first
    out_ref[:, PIECE:] = rest[:, : out_ref.shape[1] - PIECE]


def class_rows(rows, classes):
    step = 1024
    return pl.pallas_call(
        class_rows_kernel,
        grid=(rows.shape[0] // step,),
        in_specs=[pl.BlockSpec((step, PIECE), lambda i: (i, rows.shape[1] // PIECE - 1))],
        out_specs=pl.BlockSpec((step // 4, classes), lambda i: (i, 0)),
        out_shape=jax.ShapeDtypeStruct((rows.shape[0] // 4, classes), F32),
        compiler_params=params(16),
        name="class_rows",
    )(rows)


def token(rows):
    return rows[:8, :128]


def exchange(rows):
    return lax.all_to_all(rows, BOTH, split_axis=0, concat_axis=0, tiled=True)


def on_device(
    features,
    hidden_weight,
    class_weight,
    req_owner,
    req_block,
    req_offset,
    hop1_counts,
    hop2_counts,
    prior_agg,
    prior_hop1,
    cotangent,
):
    outer, inner = lax.axis_size("gx"), lax.axis_size("gy")
    want, node = route(req_owner.reshape(1, -1), req_block, req_offset, hop2_counts)
    asked = lax.all_to_all(
        lax.all_to_all(
            want.reshape(outer, inner, LANES_CAP), "gx", split_axis=0, concat_axis=0, tiled=True
        ),
        "gy",
        split_axis=1,
        concat_axis=1,
        tiled=True,
    ).reshape(DEVICES, LANES_CAP)
    feat, classes = features.shape[1], class_weight.shape[1]
    nodes = hop2_counts.shape[1]
    first = node[:, :FIRST].reshape(1, -1)
    tail = node[:, FIRST:CAP]
    folded = jnp.concatenate([tail, tail], axis=1).reshape(1, -1)
    last = jnp.pad(node[:, CAP - 2 : CAP], ((0, 0), (0, 6))).reshape(1, -1)

    picked = gather(0, asked, features, token(asked))
    part0 = exchange(picked)
    core = (lax.axis_index("gx") % CORES).reshape(1)
    x = (lax.axis_index("gy") // Y).reshape(1)
    kept, sent = backward(
        core, prior_agg, prior_hop1, cotangent, hidden_weight, class_weight, token(picked)
    )
    own, *sent = split(x, kept, swap(sent, "gx", 1))
    got = [swap(rows, "gy", Y * k) for k, rows in enumerate(sent, 1)]
    picked = ride_sums(own, got, gather(1, asked, features, token(own)))
    part1 = exchange(picked)
    sums = sum_slots(first, part0, nodes)
    picked = gather(2, asked, features, token(picked))
    own, tile = own_sums(part1)
    part2 = exchange(ride_class(tile, picked, token(sums)))
    hidden_grad = own[: 2 * feat // PIECE].reshape(-1, 2, PIECE).transpose(0, 2, 1).reshape(-1, 2)
    pre, sums = sum_folded(folded, part1, sums, hop2_counts, hidden_weight)
    class_grad = class_rows(part2, classes)
    logits = forward(
        first, last, part2, sums, pre, hop1_counts, hop2_counts, hidden_weight, class_weight
    )
    return (logits, hidden_grad, class_grad)


def solution(mesh):
    placed = (
        P(BOTH, None),
        P(),
        P(),
        P(BOTH, None, None),
        P(BOTH, None),
        P(BOTH, None),
        P(BOTH, None),
        P(BOTH, None),
        P(BOTH, None),
        P(BOTH, None),
        P(BOTH, None),
    )
    return jax.shard_map(
        on_device,
        mesh=mesh,
        in_specs=placed,
        out_specs=(P(BOTH, None), P(None, BOTH), P()),
        check_vma=False,
    )
```

time: 750 us -> 367 us (0.49)
  waiting for transfers between devices: 593 us -> 165 us
  Pallas kernels: 58.5 us -> 82.8 us
  starting transfers between devices: 24.9 us -> 45.4 us
  local copies, waits for them, and re-layouts: 17.5 us -> 34 us
  between operations: 16.3 us -> 1.02 us
    psum x1 -> x0, waiting for transfers between devices: 233 us -> none  [on_device(): class_grad = lax.psum(class_term, BOTH)]
    unnamed x4 -> x0, waiting for transfers between devices: 152 us -> none
    reduce_scatter x1 -> x0, waiting for transfers between devices: 86.6 us -> none  [on_device(): lax.psum_scatter(hidden_term, 'gx', scatter_dimension=0, tiled=True)]
    pallas_call x4 -> x11, Pallas kernels: 38.5 us -> 66 us  [the longest x3 26 us: gather(): pl.pallas_call(lambda *refs: gather_kernel(part, *refs), grid=(DEVICES //...]
    all_to_all x2 -> x3, waiting for transfers between devices: 122 us -> 147 us  [exchange(): return lax.all_to_all(rows, BOTH, split_axis=0, concat_axis=0, tiled=True)]
    ppermute x0 -> x4, waiting for transfers between devices: none -> 18.7 us  [swap(): return lax.ppermute(rows, axis, [(i, i ^ bit) for i in range(size)])]
    unnamed x27 -> x69, local copies, waits for them, and re-layouts: 13.5 us -> 31 us
    ppermute x0 -> x4, starting transfers between devices: none -> 12.7 us  [swap(): return lax.ppermute(rows, axis, [(i, i ^ bit) for i in range(size)])]
  transfers between devices with their start and end apart: 5 -> 7, of which waited for: 4 -> 6; matrix products, arithmetic and copies ran while one was open for 1% -> 2% of each run, Pallas kernels for 4% -> 15%
where the time goes in v2:
time: 367 us; the launch traced here: 366 us
  waiting for transfers between devices  165 us (45%)
  Pallas kernels  82.8 us (23%)
  starting transfers between devices  45.4 us (12%)
  blocking collectives  35.7 us (10%)
  local copies, waits for them, and re-layouts  34 us (9%)
    all_to_all x3, waiting for transfers between devices, exchange(): return lax.all_to_all(rows, BOTH, split_axis=0, concat_axis=0, tiled=True)  147 us
    all_to_all x3, starting transfers between devices, exchange(): return lax.all_to_all(rows, BOTH, split_axis=0, concat_axis=0, tiled=True)  32.8 us
    unnamed x69, local copies, waits for them, and re-layouts  31 us
    pallas_call x3, Pallas kernels, gather(): pl.pallas_call(lambda *refs: gather_kernel(part, *refs), grid=(DEVICES //...  26 us
    ppermute x4, waiting for transfers between devices, swap(): return lax.ppermute(rows, axis, [(i, i ^ bit) for i in range(size)])  18.7 us
    all_to_all x1, blocking collectives, on_device(): lax.all_to_all(want.reshape(outer, inner, LANES_CAP), 'gx', split_axis=0,...  17.9 us
    all_to_all x1, blocking collectives, on_device(): lax.all_to_all(lax.all_to_all(want.reshape(outer, inner, LANES_CAP), 'gx'...  17.8 us
    ppermute x4, starting transfers between devices, swap(): return lax.ppermute(rows, axis, [(i, i ^ bit) for i in range(size)])  12.7 us
  transfers between devices with their start and end apart: 7, of which 6 were waited for; matrix products, arithmetic and copies ran while one was open for 2% of the time, Pallas kernels for 15%

profile of v2, /device:TPU:16, one launch (start us, length us, event | category | flops | bytes accessed | tf_op | source)
XLA Modules:
  0.0 365.8 jit_solution(11863623203062355014)
XLA Ops:
  3.4 5.3 %route.1 = (s32[512,16]{1,0:T(8,128)S(1)}, s32[512,16]{1,0:T(8,128)S(1)}) custom-call(s32[1,3072]{1,0:T(1,128)S(1)} %bitcast.37, s32[1,3072]{1,0:T(1,128)S(1)} %copy-done.22, s32[1,3072]{1,0:T(1,128)S(1)} %copy-done.23, s32[1,768]{1,0:T(1,128)S(1)} %copy-done.24), custom_call_target="tpu_custom_call" | custom-call | flops 4000000000 | bytes 200000 | tf_op jit(solution)/shard_map/route/pallas_call | solution.py:84
  9.0 17.9 %all_to_all.43 = s32[16,1,512]{2,1,0:T(1,128)S(1)} all-to-all(s32[16,1,512]{2,1,0:T(1,128)S(1)} %reshape.52), channel_id=1, replica_groups=mesh['gx'=16,'gy'=32] {'gx'}, dimensions={0} | all-to-all | bytes 65536 | tf_op jit(solution)/shard_map/all_to_all | solution.py:571
  28.6 17.8 %all_to_all.44 = s32[32,1,256]{2,1,0:T(1,128)S(1)} all-to-all(s32[32,1,256]{2,1,0:T(1,128)S(1)} %reshape.54), channel_id=1, replica_groups=mesh['gx'=16,'gy'=32] {'gy'}, dimensions={0} | all-to-all | bytes 65536 | tf_op jit(solution)/shard_map/all_to_all | solution.py:570
  47.4 7.1 %gather_0.1 = bf16[4096,384]{1,0:T(8,128)(2,1)} custom-call(s32[512,16]{1,0:T(8,128)S(1)} %bitcast.32, bf16[1024,768]{1,0:T(8,128)(2,1)S(1)} %copy-done.15, s32[8,16]{1,0:T(8,128)S(1)} %slice.36.refs_2_), custom_call_target="tpu_custom_call" | custom-call | flops 3221225472 | bytes 3145728 | tf_op jit(solution)/shard_map/gather_0/pallas_call | solution.py:133
  54.5 10.6 %all-to-all-start.3 = ((bf16[512,8,384]{2,1,0:T(8,128)(2,1)}), bf16[512,8,384]{2,1,0:T(8,128)(2,1)S(1)}, u32[]{:S(2)}, u32[]{:S(2)}) async-start(bf16[512,8,384]{2,1,0:T(8,128)(2,1)} %bitcast.7), calls=%async_computation.3 | async-start | bytes 6291456 | tf_op jit(solution)/shard_map/all_to_all | solution.py:552
  72.5 8.8 %backward.1 = (f32[1024,512]{1,0:T(8,128)S(1)}, f32[1024,512]{1,0:T(8,128)}) custom-call(s32[1]{0:T(128)} %bitcast.2.core_ref, bf16[768,768]{1,0:T(8,128)(2,1)S(1)} %copy-done.20, s32[1,256]{1,0:T(1,128)S(1)} %copy-done.26, bf16[256,153]{1,0:T(8,128)(2,1)S(1)} %copy.43.cot_ref, bf16[768,1024]{1,0:T(8,128)(2,1)S(1)} %copy-done.18, ...), custom_call_target="tpu_custom_call" | custom-call | flops 2415919104 | bytes 6291456 | tf_op jit(solution)/shard_map/backward/pallas_call | solution.py:375
  84.7 4.3 %collective-permute-done.got_ref = f32[1024,512]{1,0:T(8,128)} collective-permute-done((f32[1024,512]{1,0:T(8,128)}, f32[1024,512]{1,0:T(8,128)}, u32[]{:S(2)}, u32[]{:S(2)}) %collective-permute-start) | collective-permute-done | bytes 2097184 | tf_op jit(solution)/shard_map/ppermute | solution.py:399
  90.6 2.7 split.1
  93.4 3.4 collective-permute-start.1
  96.8 4.6 %collective-permute-start.2 = (bf16[1024,128]{1,0:T(8,128)(2,1)S(1)}, bf16[1024,128]{1,0:T(8,128)(2,1)S(1)}, u32[]{:S(2)}, u32[]{:S(2)}) collective-permute-start(bf16[1024,128]{1,0:T(8,128)(2,1)S(1)} %get-tuple-element.21), channel_id=1, source_target_pairs={{0,16},{1,17},{2,18},{3,19},{4,20},{5,21},{6,22},{7,23},{8,24},{9,... | collective-permute-start | bytes 786440 | tf_op jit(solution)/shard_map/ppermute | solution.py:399
  104.0 9.4 %gather_1.1.refs_3_ = bf16[4096,384]{1,0:T(8,128)(2,1)} custom-call(s32[512,16]{1,0:T(8,128)S(1)} %bitcast.33, bf16[1024,768]{1,0:T(8,128)(2,1)S(1)} %copy-done.16, f32[8,128]{1,0:T(8,128)S(1)} %slice.31.refs_2_), custom_call_target="tpu_custom_call" | custom-call | flops 6442450944 | bytes 3145728 | tf_op jit(solution)/shard_map/gather_1/pallas_call | solution.py:133
  113.4 8.4 %collective-permute-done.2.refs_1_ = bf16[1024,128]{1,0:T(8,128)(2,1)S(1)} collective-permute-done((bf16[1024,128]{1,0:T(8,128)(2,1)S(1)}, bf16[1024,128]{1,0:T(8,128)(2,1)S(1)}, u32[]{:S(2)}, u32[]{:S(2)}) %collective-permute-start.2) | collective-permute-done | bytes 262176 | tf_op jit(solution)/shard_map/ppermute | solution.py:399
  121.8 6.0 %collective-permute-done.3.refs_2_ = bf16[1024,128]{1,0:T(8,128)(2,1)S(1)} collective-permute-done((bf16[1024,128]{1,0:T(8,128)(2,1)S(1)}, bf16[1024,128]{1,0:T(8,128)(2,1)S(1)}, u32[]{:S(2)}, u32[]{:S(2)}) %collective-permute-start.3) | collective-permute-done | bytes 262176 | tf_op jit(solution)/shard_map/ppermute | solution.py:399
  127.8 6.0 %ride_sums.1 = bf16[4096,384]{1,0:T(8,128)(2,1)} custom-call(f32[1024,128]{1,0:T(8,128)S(1)} %get-tuple-element.19.own_ref, bf16[1024,128]{1,0:T(8,128)(2,1)S(1)} %collective-permute-done.1.refs_0_, bf16[1024,128]{1,0:T(8,128)(2,1)S(1)} %collective-permute-done.2.refs_1_, ...), custom_call_target="tpu_custom_call", output_to_operand_aliasing={{}: (4, {})} | custom-call | tf_op jit(solution)/shard_map/ride_sums/pallas_call | solution.py:445
  133.8 8.4 %all-to-all-done.3 = bf16[512,8,384]{2,1,0:T(8,128)(2,1)S(1)} async-done(((bf16[512,8,384]{2,1,0:T(8,128)(2,1)}), bf16[512,8,384]{2,1,0:T(8,128)(2,1)S(1)}, u32[]{:S(2)}, u32[]{:S(2)}) %all-to-all-start.3) | async-done | bytes 3145760 | tf_op jit(solution)/shard_map/all_to_all | solution.py:552
  143.9 10.2 %all-to-all-start.2 = ((bf16[512,8,384]{2,1,0:T(8,128)(2,1)}), bf16[512,8,384]{2,1,0:T(8,128)(2,1)S(1)}, u32[]{:S(2)}, u32[]{:S(2)}) async-start(bf16[512,8,384]{2,1,0:T(8,128)(2,1)} %bitcast.5), calls=%async_computation.2 | async-start | bytes 6291456 | tf_op jit(solution)/shard_map/all_to_all | solution.py:552
  157.3 9.5 %gather_2.1.rows_ref = bf16[4096,512]{1,0:T(8,128)(2,1)S(1)} custom-call(s32[512,16]{1,0:T(8,128)S(1)} %bitcast.34, bf16[1024,768]{1,0:T(8,128)(2,1)S(1)} %copy-done.17, bf16[8,128]{1,0:T(8,128)(2,1)S(1)} %slice.38.refs_2_), custom_call_target="tpu_custom_call" | custom-call | flops 6442450944 | bytes 4194304 | tf_op jit(solution)/shard_map/gather_2/pallas_call | solution.py:133
  168.8 4.4 %sum_slots.1.sums_ref = f32[768,384]{1,0:T(8,128)S(1)} custom-call(s32[1,4096]{1,0:T(1,128)S(1)} %reshape.43.node_ref, bf16[4096,384]{1,0:T(8,128)(2,1)S(1)} %bitcast.29), custom_call_target="tpu_custom_call" | custom-call | flops 2415919104 | bytes 3145728 | tf_op jit(solution)/shard_map/sum_slots/pallas_call | solution.py:182
  174.2 56.9 %all-to-all-done.2 = bf16[512,8,384]{2,1,0:T(8,128)(2,1)S(1)} async-done(((bf16[512,8,384]{2,1,0:T(8,128)(2,1)}), bf16[512,8,384]{2,1,0:T(8,128)(2,1)S(1)}, u32[]{:S(2)}, u32[]{:S(2)}) %all-to-all-start.2) | async-done | bytes 3145760 | tf_op jit(solution)/shard_map/all_to_all | solution.py:552
  237.3 12.0 %all-to-all-start.4 = ((bf16[512,8,512]{2,1,0:T(8,128)(2,1)}), bf16[512,8,512]{2,1,0:T(8,128)(2,1)}, u32[]{:S(2)}, u32[]{:S(2)}) async-start(bf16[512,8,512]{2,1,0:T(8,128)(2,1)} %bitcast.26), calls=%async_computation.4 | async-start | bytes 8388608 | tf_op jit(solution)/shard_map/all_to_all | solution.py:552
  252.0 12.6 %sum_folded.1 = (f32[768,1024]{1,0:T(8,128)}, f32[768,384]{1,0:T(8,128)S(1)}) custom-call(s32[1,4096]{1,0:T(1,128)S(1)} %reshape.49.node_ref, bf16[4096,384]{1,0:T(8,128)(2,1)} %bitcast.28, f32[768,384]{1,0:T(8,128)S(1)} %copy-done.14, s32[1,768]{1,0:T(1,128)S(1)} %copy-done.25, bf16[768,1024]{1,0:T(8,128)(2,1)S(1)} %copy-done.19), custom_call_target="tpu_custom_call" | custom-call | flops 4831838208 | bytes 3145728 | tf_op jit(solution)/shard_map/sum_folded/pallas_call | solution.py:227
  265.7 81.3 %all-to-all-done.4 = bf16[512,8,512]{2,1,0:T(8,128)(2,1)} async-done(((bf16[512,8,512]{2,1,0:T(8,128)(2,1)}), bf16[512,8,512]{2,1,0:T(8,128)(2,1)}, u32[]{:S(2)}, u32[]{:S(2)}) %all-to-all-start.4) | async-done | bytes 4194336 | tf_op jit(solution)/shard_map/all_to_all | solution.py:552
  347.0 4.0 %class_rows.1 = f32[1024,153]{1,0:T(8,128)S(1)} custom-call(bf16[4096,512]{1,0:T(8,128)(2,1)} %bitcast.10.rows_ref), custom_call_target="tpu_custom_call" | custom-call | tf_op jit(solution)/shard_map/class_rows/pallas_call | solution.py:536
  353.5 11.5 %forward.1 = f32[256,153]{1,0:T(8,128)S(1)} custom-call(s32[1,4096]{1,0:T(1,128)S(1)} %reshape.43.node_ref, s32[1,4096]{1,0:T(1,128)S(1)} %reshape.44.last_ref, bf16[4096,512]{1,0:T(8,128)(2,1)} %bitcast.10.rows_ref, f32[768,384]{1,0:T(8,128)S(1)} %copy-done.29, f32[768,1024]{1,0:T(8,128)} %get-tuple-element.25.pre_ref, s32[1,256]{1,0:T(1,128)S(1)} %copy-done.27, ...), custom_call_target="tpu_custom_call" | custom-call | flops 3019898880 | bytes 3145728 | tf_op jit(solution)/shard_map/forward/pallas_call | solution.py:302
  (94 shorter events, 41.6 us)
Async XLA Ops:
  3.4 43.9 %copy-start.15 = (bf16[1024,768]{1,0:T(8,128)(2,1)S(1)}, bf16[1024,768]{1,0:T(8,128)(2,1)}, u32[]{:S(2)}) copy-start(bf16[1024,768]{1,0:T(8,128)(2,1)} %refs_1_.5) | copy-start | bytes 4718596
  47.3 7.2 %copy-start.10 = (s32[16,32,16]{2,1,0:T(8,128)}, s32[16,32,16]{2,1,0:T(8,128)S(1)}, u32[]{:S(2)}) copy-start(s32[16,32,16]{2,1,0:T(8,128)S(1)} %copy.42) | copy-start | bytes 98308
  54.5 14.3 %copy-start.26 = (s32[1,256]{1,0:T(1,128)S(1)}, s32[1,256]{1,0:T(1,128)}, u32[]{:S(2)}) copy-start(s32[1,256]{1,0:T(1,128)} %hop1_ref.2) | copy-start | bytes 3076
  54.5 87.7 %all-to-all-start.3 = ((bf16[512,8,384]{2,1,0:T(8,128)(2,1)}), bf16[512,8,384]{2,1,0:T(8,128)(2,1)S(1)}, u32[]{:S(2)}, u32[]{:S(2)}) async-start(bf16[512,8,384]{2,1,0:T(8,128)(2,1)} %bitcast.7), calls=%async_computation.3 | async-start | bytes 6291456 | tf_op jit(solution)/shard_map/all_to_all | solution.py:552
  82.7 6.4 %collective-permute-start = (f32[1024,512]{1,0:T(8,128)}, f32[1024,512]{1,0:T(8,128)}, u32[]{:S(2)}, u32[]{:S(2)}) collective-permute-start(f32[1024,512]{1,0:T(8,128)} %get-tuple-element.18), channel_id=1, source_target_pairs={{0,32},{32,0},{64,96},{96,64},{128,160},{160,128},{192,224},{224,1... | collective-permute-start | bytes 6291464 | tf_op jit(solution)/shard_map/ppermute | solution.py:399
  89.0 1.6 copy-start.7
  90.6 13.4 %copy-start.11 = (s32[16,32,16]{2,1,0:T(8,128)S(1)}, s32[16,32,16]{2,1,0:T(8,128)}, u32[]{:S(2)}) copy-start(s32[16,32,16]{2,1,0:T(8,128)} %copy-done.10) | copy-start | bytes 98308
  90.6 13.4 %copy-start.16 = (bf16[1024,768]{1,0:T(8,128)(2,1)S(1)}, bf16[1024,768]{1,0:T(8,128)(2,1)}, u32[]{:S(2)}) copy-start(bf16[1024,768]{1,0:T(8,128)(2,1)} %refs_1_.5) | copy-start | bytes 4718596
  93.4 20.1 %collective-permute-start.1 = (bf16[1024,128]{1,0:T(8,128)(2,1)S(1)}, bf16[1024,128]{1,0:T(8,128)(2,1)S(1)}, u32[]{:S(2)}, u32[]{:S(2)}) collective-permute-start(bf16[1024,128]{1,0:T(8,128)(2,1)S(1)} %get-tuple-element.20), channel_id=1, source_target_pairs={{0,8},{1,9},{2,10},{3,11},{4,12},{5,13},{6,14},{7,15},{8,0},{9,1},... | collective-permute-start | bytes 786440 | tf_op jit(solution)/shard_map/ppermute | solution.py:399
  96.8 25.1 %collective-permute-start.2 = (bf16[1024,128]{1,0:T(8,128)(2,1)S(1)}, bf16[1024,128]{1,0:T(8,128)(2,1)S(1)}, u32[]{:S(2)}, u32[]{:S(2)}) collective-permute-start(bf16[1024,128]{1,0:T(8,128)(2,1)S(1)} %get-tuple-element.21), channel_id=1, source_target_pairs={{0,16},{1,17},{2,18},{3,19},{4,20},{5,21},{6,22},{7,23},{8,24},{9,... | collective-permute-start | bytes 786440 | tf_op jit(solution)/shard_map/ppermute | solution.py:399
  101.4 26.4 %collective-permute-start.3 = (bf16[1024,128]{1,0:T(8,128)(2,1)S(1)}, bf16[1024,128]{1,0:T(8,128)(2,1)S(1)}, u32[]{:S(2)}, u32[]{:S(2)}) collective-permute-start(bf16[1024,128]{1,0:T(8,128)(2,1)S(1)} %get-tuple-element.22), channel_id=1, source_target_pairs={{0,24},{1,25},{2,26},{3,27},{4,28},{5,29},{6,30},{7,31},{8,16},{9,... | collective-permute-start | bytes 786440 | tf_op jit(solution)/shard_map/ppermute | solution.py:399
  142.2 1.8 copy-start.4
  143.9 87.2 %all-to-all-start.2 = ((bf16[512,8,384]{2,1,0:T(8,128)(2,1)}), bf16[512,8,384]{2,1,0:T(8,128)(2,1)S(1)}, u32[]{:S(2)}, u32[]{:S(2)}) async-start(bf16[512,8,384]{2,1,0:T(8,128)(2,1)} %bitcast.5), calls=%async_computation.2 | async-start | bytes 6291456 | tf_op jit(solution)/shard_map/all_to_all | solution.py:552
  157.3 11.5 %copy-start.5 = (bf16[512,8,384]{2,1,0:T(8,128)(2,1)S(1)}, bf16[512,8,384]{2,1,0:T(8,128)(2,1)}, u32[]{:S(2)}) copy-start(bf16[512,8,384]{2,1,0:T(8,128)(2,1)} %copy-done.4) | copy-start | bytes 9437188
  166.8 2.0 copy-start
  231.1 4.1 %copy-start.3 = (bf16[512,8,384]{2,1,0:T(8,128)(2,1)}, bf16[512,8,384]{2,1,0:T(8,128)(2,1)S(1)}, u32[]{:S(2)}) copy-start(bf16[512,8,384]{2,1,0:T(8,128)(2,1)S(1)} %all-to-all-done.2) | copy-start | bytes 9437188
  231.8 2.6 copy-start.1
  235.2 2.0 copy-start.2
  237.3 13.4 %copy-start.14 = (f32[768,384]{1,0:T(8,128)S(1)}, f32[768,384]{1,0:T(8,128)}, u32[]{:S(2)}) copy-start(f32[768,384]{1,0:T(8,128)} %copy-done.13) | copy-start | bytes 3538948
  237.3 13.4 %copy-start.25 = (s32[1,768]{1,0:T(1,128)S(1)}, s32[1,768]{1,0:T(1,128)}, u32[]{:S(2)}) copy-start(s32[1,768]{1,0:T(1,128)} %hop2_ref.5) | copy-start | bytes 9220
  237.3 109.7 %all-to-all-start.4 = ((bf16[512,8,512]{2,1,0:T(8,128)(2,1)}), bf16[512,8,512]{2,1,0:T(8,128)(2,1)}, u32[]{:S(2)}, u32[]{:S(2)}) async-start(bf16[512,8,512]{2,1,0:T(8,128)(2,1)} %bitcast.26), calls=%async_computation.4 | async-start | bytes 8388608 | tf_op jit(solution)/shard_map/all_to_all | solution.py:552
  250.6 1.4 copy-start.19
  347.0 5.2 %copy-start.9 = (bf16[1024,153]{1,0:T(8,128)(2,1)S(1)}, bf16[1024,153]{1,0:T(8,128)(2,1)}, u32[]{:S(2)}) copy-start(bf16[1024,153]{1,0:T(8,128)(2,1)} %copy.44.w2_ref) | copy-start | bytes 940036
  347.0 5.2 %copy-start.27 = (s32[1,256]{1,0:T(1,128)S(1)}, s32[1,256]{1,0:T(1,128)}, u32[]{:S(2)}) copy-start(s32[1,256]{1,0:T(1,128)} %hop1_ref.3) | copy-start | bytes 3076
  (13 other events, 13.6 us)

commit v3 on v2

--- a/solution.py
+++ b/solution.py
@@ -11,6 +11,7 @@
 LANES_CAP = 16
 FIRST = 8
 PIECE = 128
+MOST_MIB = 60
 BOTH = ("gx", "gy")
 Z, CORES, X, Y = 8, 2, 4, 8
 F32 = jnp.float32
@@ -84,7 +85,7 @@
     return pl.pallas_call(
         route_kernel,
         out_shape=(shape, shape),
-        compiler_params=pltpu.CompilerParams(vmem_limit_bytes=32 * MIB),
+        compiler_params=pltpu.CompilerParams(vmem_limit_bytes=MOST_MIB * MIB),
         cost_estimate=pl.CostEstimate(flops=4_000_000_000, bytes_accessed=200_000, transcendentals=0),
         name="route",
     )(owners, blocks, offsets, hop2)
@@ -125,7 +126,7 @@
     held, width = features.shape
     half = width // 2
     sent = half + PIECE if part == 2 else half
-    readers = 64
+    readers = 128
     if part == 1:
         source = pl.BlockSpec((held, width), lambda i: (0, 0))
     else:
@@ -140,7 +141,7 @@
         ],
         out_specs=pl.BlockSpec((readers * 8, sent), lambda i: (i, 0)),
         out_shape=jax.ShapeDtypeStruct((DEVICES * 8, sent), BF16),
-        compiler_params=params(32),
+        compiler_params=params(MOST_MIB),
         cost_estimate=pl.CostEstimate(
             flops=2 * DEVICES * 8 * held * (half if part == 0 else width),
             bytes_accessed=DEVICES * 16 * sent,
@@ -188,7 +189,7 @@
         ],
         out_specs=pl.BlockSpec((nodes, half), lambda i: (0, 0)),
         out_shape=jax.ShapeDtypeStruct((nodes, half), F32),
-        compiler_params=params(32),
+        compiler_params=params(MOST_MIB),
         cost_estimate=pl.CostEstimate(
             flops=2 * nodes * count * half, bytes_accessed=count * half * 2, transcendentals=0
         ),
@@ -203,7 +204,20 @@
     return 1.0 + jnp.sum(counts, axis=1, keepdims=True)
 
 
-def sum_folded_kernel(node_ref, rows_ref, sums_ref, hop2_ref, w1_ref, pre_ref, high_ref, low_ref):
+def sum_folded_kernel(
+    node_ref,
+    rows_ref,
+    sums_ref,
+    hop1_ref,
+    hop2_ref,
+    w1_ref,
+    pre_ref,
+    high_ref,
+    groups_ref,
+    sizes1_ref,
+    sizes2_ref,
+    low_ref,
+):
     nodes, half = sums_ref.shape
     takes = taken(node_ref, nodes)
     low = (iota(takes.shape, 1) & 7) < 4
@@ -216,14 +230,24 @@
 
     @pl.when(pl.program_id(0) == pl.num_programs(0) - 1)
     def _():
-        agg = ((sums_ref[...] + low_ref[...]) / group_sizes(hop2_ref)).astype(BF16)
+        sizes2 = group_sizes(hop2_ref)
+        sizes2_ref[...] = sizes2
+        groups_ref[...], sizes1_ref[...] = seed_groups(hop1_ref[...].astype(F32), nodes)
+        agg = ((sums_ref[...] + low_ref[...]) / sizes2).astype(BF16)
         pre_ref[...] = dot(agg, w1_ref[...])
 
 
-def sum_folded(node, rows, sums, hop2, w1):
+def sum_folded(node, rows, sums, hop1, hop2, w1):
     step = 1024
     count, half = rows.shape
-    nodes, hid = sums.shape[0], w1.shape[1]
+    nodes, hid, seeds = sums.shape[0], w1.shape[1], hop1.shape[1]
+    given = [
+        jax.ShapeDtypeStruct((nodes, hid), F32),
+        jax.ShapeDtypeStruct((nodes, half), F32),
+        jax.ShapeDtypeStruct((seeds, nodes), BF16),
+        jax.ShapeDtypeStruct((seeds, 1), F32),
+        jax.ShapeDtypeStruct((nodes, 1), F32),
+    ]
     return pl.pallas_call(
         sum_folded_kernel,
         grid=(count // step,),
@@ -231,24 +255,19 @@
             pl.BlockSpec((1, step), lambda i: (0, i)),
             pl.BlockSpec((step, half), lambda i: (i, 0)),
             whole(sums),
+            whole(hop1),
             whole(hop2),
             pl.BlockSpec((half, hid), lambda i: (0, 0)),
         ],
-        out_specs=(
-            pl.BlockSpec((nodes, hid), lambda i: (0, 0)),
-            pl.BlockSpec((nodes, half), lambda i: (0, 0)),
-        ),
-        out_shape=(
-            jax.ShapeDtypeStruct((nodes, hid), F32),
-            jax.ShapeDtypeStruct((nodes, half), F32),
-        ),
+        out_specs=[whole(a) for a in given],
+        out_shape=given,
         scratch_shapes=[pltpu.VMEM((nodes, half), F32)],
-        compiler_params=params(48),
+        compiler_params=params(MOST_MIB),
         cost_estimate=pl.CostEstimate(
             flops=4 * nodes * count * half, bytes_accessed=count * half * 2, transcendentals=0
         ),
         name="sum_folded",
-    )(node, rows, sums, hop2, w1)
+    )(node, rows, sums, hop1, hop2, w1)
 
 
 def seed_groups(counts, nodes):
@@ -268,62 +287,96 @@
     rows_ref,
     sums_ref,
     pre_ref,
-    hop1_ref,
-    hop2_ref,
+    groups_ref,
+    sizes1_ref,
+    sizes2_ref,
     w1_ref,
     w2_ref,
     out_ref,
+    class_ref,
     acc_ref,
+    pre_all,
+    w1_all,
 ):
     nodes, half = sums_ref.shape
+    block = pre_ref.shape[1]
+    pre_all[pl.program_id(0)] = pre_ref[...]
+    w1_all[pl.program_id(0)] = w1_ref[...]
     add_up(acc_ref, dot(zero_one(taken(node_ref, nodes)), rows_ref[:, :half]))
-    acc_ref[:, half - PIECE :] += dot(zero_one(taken(last_ref, nodes)), rows_ref[:, half:])
+    tile = rows_ref[:, half:]
+    count = tile.shape[0]
+    shape = count // 4, count
+    j, i = iota(shape, 0), iota(shape, 1)
+    same, odd, sub = (i >> 3) == (j >> 1), j & 1, i & 7
+    last = dot(zero_one(same & (sub == odd)), tile).astype(BF16)
+    acc_ref[:, half - PIECE :] += dot(zero_one(taken(last_ref, nodes)), last)
+
+    first = zero_one(same & ((sub == 2 + odd) | (sub == 4 + odd)))
+    class_ref[:PIECE, :] = dot(tile, first, ((0,), (1,)))
+    rest = dot(tile, zero_one(same & (sub == 6)), ((0,), (1,)))
+    rest = rest[:64] + rest[64:]
+    more = class_ref.shape[0] - PIECE
+    odd = (iota((more, count // 4), 1) & 1) == 1
+    class_ref[PIECE:, :] = jnp.where(odd, rest[32 : 32 + more], rest[:more])
 
     @pl.when(pl.program_id(0) == pl.num_programs(0) - 1)
     def _():
-        agg_one = ((sums_ref[...] + acc_ref[...]) / group_sizes(hop2_ref)).astype(BF16)
-        groups, sizes = seed_groups(hop1_ref[...].astype(F32), nodes)
-        scale = 1.0 / sizes
+        agg_one = ((sums_ref[...] + acc_ref[...]) / sizes2_ref[...]).astype(BF16)
+        groups = groups_ref[...]
+        scale = 1.0 / sizes1_ref[...]
         total = jnp.zeros(out_ref.shape, F32)
-        for at in range(0, w1_ref.shape[1], 256):
-            pre = pre_ref[:, at : at + 256] + dot(agg_one, w1_ref[:, at : at + 256])
+        for k in range(pre_all.shape[0]):
+            pre = pre_all[k] + dot(agg_one, w1_all[k])
             hidden = (pre * jax.nn.sigmoid(pre)).astype(BF16)
             agg_two = (dot(groups, hidden) * scale).astype(BF16)
-            total = total + dot(agg_two, w2_ref[at : at + 256, :])
+            mine = slice(k * block, (k + 1) * block)
+            total = total + dot(w2_ref[:, mine], agg_two, ((1,), (1,)))
         out_ref[...] = total
 
 
-def forward(node, last, rows, sums, pre, hop1, hop2, w1, w2):
+def forward(node, last, rows, sums, pre, groups, sizes1, sizes2, w1, w2):
     step = 1024
     count, sent = rows.shape
     nodes, half = sums.shape
     hid = w1.shape[1]
-    seeds, classes = hop1.shape[1], w2.shape[1]
+    seeds, classes = groups.shape[0], w2.shape[0]
+    steps = count // step
     return pl.pallas_call(
         forward_kernel,
-        grid=(count // step,),
+        grid=(steps,),
         in_specs=[
             pl.BlockSpec((1, step), lambda i: (0, i)),
-            pl.BlockSpec((1, step), lambda i: (0, i)),
+            pl.BlockSpec((1, step // 4), lambda i: (0, i)),
             pl.BlockSpec((step, sent), lambda i: (i, 0)),
             whole(sums),
-            whole(pre),
-            whole(hop1),
-            whole(hop2),
-            pl.BlockSpec((half, hid), lambda i: (1, 0)),
+            pl.BlockSpec((nodes, hid // steps), lambda i: (0, i)),
+            whole(groups),
+            whole(sizes1),
+            whole(sizes2),
+            pl.BlockSpec((half, hid // steps), lambda i: (1, i)),
             whole(w2),
         ],
-        out_specs=pl.BlockSpec((seeds, classes), lambda i: (0, 0)),
-        out_shape=jax.ShapeDtypeStruct((seeds, classes), F32),
-        scratch_shapes=[pltpu.VMEM((nodes, half), F32)],
-        compiler_params=params(48),
+        out_specs=[
+            pl.BlockSpec((classes, seeds), lambda i: (0, 0)),
+            pl.BlockSpec((classes, step // 4), lambda i: (0, i)),
+        ],
+        out_shape=[
+            jax.ShapeDtypeStruct((classes, seeds), F32),
+            jax.ShapeDtypeStruct((classes, count // 4), F32),
+        ],
+        scratch_shapes=[
+            pltpu.VMEM((nodes, half), F32),
+            pltpu.VMEM((steps, nodes, hid // steps), F32),
+            pltpu.VMEM((steps, half, hid // steps), BF16),
+        ],
+        compiler_params=params(MOST_MIB),
         cost_estimate=pl.CostEstimate(
             flops=2 * nodes * count * half + 2 * nodes * half * hid,
-            bytes_accessed=count * half * 2,
+            bytes_accessed=count * sent * 2,
             transcendentals=nodes * hid,
         ),
         name="forward",
-    )(node, last, rows, sums, pre, hop1, hop2, w1, w2)
+    )(node, last, rows, sums, pre, groups, sizes1, sizes2, w1, w2)
 
 
 def backward_kernel(
@@ -343,17 +396,17 @@
     hands = grouped | (seed == node)
     node_scale = jnp.sum(jnp.where(hands, 1.0 / (1.0 + counts), 0.0), axis=1, keepdims=True)
     cot = cot_ref[...]
-    node_cot = dot(jnp.where(hands, 1.0, 0.0).astype(BF16), cot).astype(BF16)
+    node_cot = dot(zero_one(hands), cot, ((1,), (1,))).astype(BF16)
 
     agg = agg_ref[...]
     pre = dot(agg, w1_ref[...])
     sigma = jax.nn.sigmoid(pre)
     hidden = (pre * sigma).astype(BF16)
     agg_two = (dot(groups, hidden) * scale).astype(BF16)
-    classes = cot.shape[1]
-    wide = zero_one(iota((classes, 2 * PIECE), 0) == iota((classes, 2 * PIECE), 1))
-    class_term = dot(agg_two, dot(cot, wide).astype(BF16), ((0,), (0,)))
-    d_hidden = dot(node_cot, w2_ref[...], ((1,), (1,))) * node_scale
+    classes = cot.shape[0]
+    wide = zero_one(iota((2 * PIECE, classes), 0) == iota((2 * PIECE, classes), 1))
+    class_term = dot(agg_two, dot(wide, cot).astype(BF16), ((0,), (1,)))
+    d_hidden = dot(node_cot, w2_ref[...]) * node_scale
     d_pre = (d_hidden * sigma * (1.0 + pre * (1.0 - sigma))).astype(BF16)
     hidden_term = dot(d_pre, agg, ((0,), (0,)))
     first = core_ref[0] == 0
@@ -369,7 +422,7 @@
 def backward(core, agg, hop1, cot, w1, w2, after):
     nodes, feat = agg.shape
     hid = w1.shape[1]
-    classes = cot.shape[1]
+    classes = cot.shape[0]
     step = 256
     half = (feat + 2 * PIECE) // 2
     return pl.pallas_call(
@@ -381,12 +434,12 @@
             whole(hop1),
             whole(cot),
             pl.BlockSpec((feat, step), lambda i: (0, i)),
-            pl.BlockSpec((step, classes), lambda i: (i, 0)),
+            pl.BlockSpec((classes, step), lambda i: (0, i)),
             pl.BlockSpec(memory_space=pl.ANY),
         ],
         out_specs=[pl.BlockSpec((step, half), lambda i: (i, 0))] * 2,
         out_shape=[jax.ShapeDtypeStruct((hid, half), F32)] * 2,
-        compiler_params=params(48),
+        compiler_params=params(MOST_MIB),
         cost_estimate=pl.CostEstimate(
             flops=4 * nodes * feat * hid, bytes_accessed=6 * MIB, transcendentals=nodes * hid
         ),
@@ -421,7 +474,7 @@
         out_specs=[pl.BlockSpec((step, PIECE), lambda i: (i, 0))] * X,
         out_shape=[jax.ShapeDtypeStruct((rows, PIECE), F32)]
         + [jax.ShapeDtypeStruct((rows, PIECE), BF16)] * (X - 1),
-        compiler_params=params(16),
+        compiler_params=params(MOST_MIB),
         name="split",
     )(x, kept, got)
 
@@ -503,7 +556,7 @@
 
 
 def ride_class(tile, rows, after):
-    step = 1024
+    step = 4096
     last = pl.BlockSpec((step, PIECE), lambda i: (i, rows.shape[1] // PIECE - 1))
     return pl.pallas_call(
         ride_class_kernel,
@@ -512,36 +565,9 @@
         out_specs=last,
         out_shape=jax.ShapeDtypeStruct(rows.shape, BF16),
         input_output_aliases={1: 0},
-        compiler_params=params(16),
+        compiler_params=params(MOST_MIB),
         name="ride_class",
     )(tile, rows, after)
-
-
-def class_rows_kernel(rows_ref, out_ref):
-    rows = rows_ref[...]
-    shape = out_ref.shape[0], rows.shape[0]
-    j, i = iota(shape, 0), iota(shape, 1)
-    sender, row, sub = (i >> 3) == (j >> 1), j & 1, i & 7
-    first = dot(zero_one(sender & ((sub == 2 + row) | (sub == 4 + row))), rows)
-    rest = dot(zero_one(sender & (sub == 6)), rows)
-    rest = rest + pltpu.roll(rest, 64, 1)
-    odd = (iota(rest.shape, 0) & 1) == 1
-    rest = jnp.where(odd, pltpu.roll(rest, 96, 1), rest)
-    out_ref[:, :PIECE] = first
-    out_ref[:, PIECE:] = rest[:, : out_ref.shape[1] - PIECE]
-
-
-def class_rows(rows, classes):
-    step = 1024
-    return pl.pallas_call(
-        class_rows_kernel,
-        grid=(rows.shape[0] // step,),
-        in_specs=[pl.BlockSpec((step, PIECE), lambda i: (i, rows.shape[1] // PIECE - 1))],
-        out_specs=pl.BlockSpec((step // 4, classes), lambda i: (i, 0)),
-        out_shape=jax.ShapeDtypeStruct((rows.shape[0] // 4, classes), F32),
-        compiler_params=params(16),
-        name="class_rows",
-    )(rows)
 
 
 def token(rows):
@@ -576,19 +602,20 @@
         concat_axis=1,
         tiled=True,
     ).reshape(DEVICES, LANES_CAP)
-    feat, classes = features.shape[1], class_weight.shape[1]
+    feat = features.shape[1]
     nodes = hop2_counts.shape[1]
     first = node[:, :FIRST].reshape(1, -1)
     tail = node[:, FIRST:CAP]
     folded = jnp.concatenate([tail, tail], axis=1).reshape(1, -1)
-    last = jnp.pad(node[:, CAP - 2 : CAP], ((0, 0), (0, 6))).reshape(1, -1)
-
-    picked = gather(0, asked, features, token(asked))
+    last = node[:, CAP - 2 : CAP].reshape(1, -1)
+    w2 = class_weight.T
+
+    picked = gather(0, asked, features, asked)
     part0 = exchange(picked)
     core = (lax.axis_index("gx") % CORES).reshape(1)
     x = (lax.axis_index("gy") // Y).reshape(1)
     kept, sent = backward(
-        core, prior_agg, prior_hop1, cotangent, hidden_weight, class_weight, token(picked)
+        core, prior_agg, prior_hop1, cotangent.T, hidden_weight, w2, token(picked)
     )
     own, *sent = split(x, kept, swap(sent, "gx", 1))
     got = [swap(rows, "gy", Y * k) for k, rows in enumerate(sent, 1)]
@@ -598,12 +625,14 @@
     picked = gather(2, asked, features, token(picked))
     own, tile = own_sums(part1)
     part2 = exchange(ride_class(tile, picked, token(sums)))
-    hidden_grad = own[: 2 * feat // PIECE].reshape(-1, 2, PIECE).transpose(0, 2, 1).reshape(-1, 2)
-    pre, sums = sum_folded(folded, part1, sums, hop2_counts, hidden_weight)
-    class_grad = class_rows(part2, classes)
-    logits = forward(
-        first, last, part2, sums, pre, hop1_counts, hop2_counts, hidden_weight, class_weight
+    hidden_grad = own[: 2 * feat // PIECE].reshape(-1, 2, PIECE).transpose(1, 0, 2).reshape(2, -1).T
+    pre, sums, *groups = sum_folded(
+        folded, part1, sums, hop1_counts, hop2_counts, hidden_weight
     )
+    logits, class_grad = forward(
+        first, last, part2, sums, pre, *groups, hidden_weight, w2
+    )
+    logits, class_grad = logits.T, class_grad.T
     return (logits, hidden_grad, class_grad)
 
 

time: 367 us -> 360 us (0.981)
  local copies, waits for them, and re-layouts: 34 us -> 17.2 us
  Pallas kernels: 82.8 us -> 90.1 us
    unnamed x69 -> x18, local copies, waits for them, and re-layouts: 31 us -> 6.46 us
    pallas_call x1, Pallas kernels: 5.98 us -> 2.02 us  [ride_sums(): pl.pallas_call(ride_sums_kernel, grid=(DEVICES // readers,), in_specs=[mi...]
    slice x5 -> x4, local copies, waits for them, and re-layouts: 1.33 us -> 5.06 us  [token(): return rows[:8, :128]]
    pallas_call x2 -> x1, Pallas kernels: 15.6 us -> 14.9 us  [forward(): pl.pallas_call(forward_kernel, grid=(steps,), in_specs=[pl.BlockSpec((1,...]
  transfers between devices with their start and end apart: 7 -> 7, of which waited for: 6 -> 6; matrix products, arithmetic and copies ran while one was open for 2% -> 2% of each run, Pallas kernels for 15% -> 16%
where the time goes in v3:
time: 360 us; the launch traced here: 359 us
  waiting for transfers between devices  166 us (46%)
  Pallas kernels  90.1 us (25%)
  starting transfers between devices  47.6 us (13%)
  blocking collectives  35.7 us (10%)
  local copies, waits for them, and re-layouts  17.2 us (5%)
    all_to_all x3, waiting for transfers between devices, exchange(): return lax.all_to_all(rows, BOTH, split_axis=0, concat_axis=0, tiled=True)  147 us
    all_to_all x3, starting transfers between devices, exchange(): return lax.all_to_all(rows, BOTH, split_axis=0, concat_axis=0, tiled=True)  34.8 us
    pallas_call x3, Pallas kernels, gather(): pl.pallas_call(lambda *refs: gather_kernel(part, *refs), grid=(DEVICES //...  28.2 us
    ppermute x4, waiting for transfers between devices, swap(): return lax.ppermute(rows, axis, [(i, i ^ bit) for i in range(size)])  18.5 us
    all_to_all x1, blocking collectives, on_device(): lax.all_to_all(want.reshape(outer, inner, LANES_CAP), 'gx', split_axis=0,...  17.9 us
    all_to_all x1, blocking collectives, on_device(): lax.all_to_all(lax.all_to_all(want.reshape(outer, inner, LANES_CAP), 'gx'...  17.8 us
    pallas_call x1, Pallas kernels, forward(): pl.pallas_call(forward_kernel, grid=(steps,), in_specs=[pl.BlockSpec((1,...  14.9 us
    pallas_call x1, Pallas kernels, sum_folded(): pl.pallas_call(sum_folded_kernel, grid=(count // step,), in_specs=[pl.Blo...  14.1 us
  transfers between devices with their start and end apart: 7, of which 6 were waited for; matrix products, arithmetic and copies ran while one was open for 2% of the time, Pallas kernels for 16%

profile of v3, /device:TPU:16, one launch (start us, length us, event | category | flops | bytes accessed | tf_op | source)
XLA Modules:
  0.0 359.0 jit_solution(13003456866372894189)
XLA Ops:
  0.6 6.8 %route.1 = (s32[512,16]{1,0:T(8,128)}, s32[512,16]{1,0:T(8,128)}) custom-call(s32[1,3072]{1,0:T(1,128)} %bitcast.48, s32[1,3072]{1,0:T(1,128)} %block_ref.1, s32[1,3072]{1,0:T(1,128)} %offset_ref.1, s32[1,768]{1,0:T(1,128)} %hop2_ref.3), custom_call_target="tpu_custom_call" | custom-call | flops 4000000000 | bytes 200000 | tf_op jit(solution)/shard_map/route/pallas_call | solution.py:85
  8.6 17.9 %all_to_all.43 = s32[16,1,512]{2,1,0:T(1,128)S(1)} all-to-all(s32[16,1,512]{2,1,0:T(1,128)S(1)} %reshape.52), channel_id=1, replica_groups=mesh['gx'=16,'gy'=32] {'gx'}, dimensions={0} | all-to-all | bytes 65536 | tf_op jit(solution)/shard_map/all_to_all | solution.py:597
  28.2 17.8 %all_to_all.44 = s32[32,1,256]{2,1,0:T(1,128)S(1)} all-to-all(s32[32,1,256]{2,1,0:T(1,128)S(1)} %reshape.54), channel_id=1, replica_groups=mesh['gx'=16,'gy'=32] {'gy'}, dimensions={0} | all-to-all | bytes 65536 | tf_op jit(solution)/shard_map/all_to_all | solution.py:596
  47.6 7.4 %gather_0.1 = bf16[4096,384]{1,0:T(8,128)(2,1)} custom-call(s32[512,16]{1,0:T(8,128)} %bitcast.40, bf16[1024,768]{1,0:T(8,128)(2,1)} %refs_1_.5, s32[512,16]{1,0:T(8,128)} %bitcast.41), custom_call_target="tpu_custom_call" | custom-call | flops 3221225472 | bytes 3145728 | tf_op jit(solution)/shard_map/gather_0/pallas_call | solution.py:134
  55.0 13.0 %all-to-all-start.3 = ((bf16[512,8,384]{2,1,0:T(8,128)(2,1)}), bf16[512,8,384]{2,1,0:T(8,128)(2,1)}, u32[]{:S(2)}, u32[]{:S(2)}) async-start(bf16[512,8,384]{2,1,0:T(8,128)(2,1)} %bitcast.31), calls=%async_computation.3 | async-start | bytes 6291456 | tf_op jit(solution)/shard_map/all_to_all | solution.py:578
  69.2 10.1 %backward.1 = (f32[1024,512]{1,0:T(8,128)}, f32[1024,512]{1,0:T(8,128)}) custom-call(s32[1]{0:T(128)} %bitcast.2.core_ref, bf16[768,768]{1,0:T(8,128)(2,1)} %agg_ref.1, s32[1,256]{1,0:T(1,128)} %hop1_ref.2, bf16[153,256]{1,0:T(8,128)(2,1)} %bitcast.47, bf16[768,1024]{1,0:T(8,128)(2,1)} %w1_ref.5, bf16[153,1024]{1,0:T(8,128)(2,1)} %bitcast.37, ...), custom_call_target="tpu_custom_call" | custom-call | flops 2415919104 | bytes 6291456 | tf_op jit(solution)/shard_map/backward/pallas_call | solution.py:428
  81.4 4.2 %collective-permute-done.got_ref = f32[1024,512]{1,0:T(8,128)S(1)} collective-permute-done((f32[1024,512]{1,0:T(8,128)}, f32[1024,512]{1,0:T(8,128)S(1)}, u32[]{:S(2)}, u32[]{:S(2)}) %collective-permute-start) | collective-permute-done | bytes 2097184 | tf_op jit(solution)/shard_map/ppermute | solution.py:452
  87.0 4.1 %split.1 = (f32[1024,128]{1,0:T(8,128)}, bf16[1024,128]{1,0:T(8,128)(2,1)}, bf16[1024,128]{1,0:T(8,128)(2,1)}, bf16[1024,128]{1,0:T(8,128)(2,1)}) custom-call(s32[1]{0:T(128)} %bitcast.1.x_ref, f32[1024,512]{1,0:T(8,128)} %get-tuple-element.22.kept_ref, f32[1024,512]{1,0:T(8,128)} %copy-done.6), custom_call_target="tpu_custom_call" | custom-call | tf_op jit(solution)/shard_map/split/pallas_call | solution.py:470
  92.4 3.4 collective-permute-start.1
  95.8 4.6 %collective-permute-start.2 = (bf16[1024,128]{1,0:T(8,128)(2,1)}, bf16[1024,128]{1,0:T(8,128)(2,1)S(1)}, u32[]{:S(2)}, u32[]{:S(2)}) collective-permute-start(bf16[1024,128]{1,0:T(8,128)(2,1)} %get-tuple-element.26), channel_id=1, source_target_pairs={{0,16},{1,17},{2,18},{3,19},{4,20},{5,21},{6,22},{7,23},{8,24},{9,... | collective-permute-start | bytes 786440 | tf_op jit(solution)/shard_map/ppermute | solution.py:452
  100.4 2.7 collective-permute-start.3
  103.2 10.2 %gather_1.1.refs_3_ = bf16[4096,384]{1,0:T(8,128)(2,1)} custom-call(s32[512,16]{1,0:T(8,128)} %bitcast.42, bf16[1024,768]{1,0:T(8,128)(2,1)} %refs_1_.5, f32[8,128]{1,0:T(8,128)} %slice.27.refs_2_), custom_call_target="tpu_custom_call" | custom-call | flops 6442450944 | bytes 3145728 | tf_op jit(solution)/shard_map/gather_1/pallas_call | solution.py:134
  113.3 7.8 %collective-permute-done.2.refs_1_ = bf16[1024,128]{1,0:T(8,128)(2,1)S(1)} collective-permute-done((bf16[1024,128]{1,0:T(8,128)(2,1)}, bf16[1024,128]{1,0:T(8,128)(2,1)S(1)}, u32[]{:S(2)}, u32[]{:S(2)}) %collective-permute-start.2) | collective-permute-done | bytes 262176 | tf_op jit(solution)/shard_map/ppermute | solution.py:452
  121.2 6.5 %collective-permute-done.3.refs_2_ = bf16[1024,128]{1,0:T(8,128)(2,1)S(1)} collective-permute-done((bf16[1024,128]{1,0:T(8,128)(2,1)}, bf16[1024,128]{1,0:T(8,128)(2,1)S(1)}, u32[]{:S(2)}, u32[]{:S(2)}) %collective-permute-start.3) | collective-permute-done | bytes 262176 | tf_op jit(solution)/shard_map/ppermute | solution.py:452
  133.3 9.9 %all-to-all-done.3 = bf16[512,8,384]{2,1,0:T(8,128)(2,1)} async-done(((bf16[512,8,384]{2,1,0:T(8,128)(2,1)}), bf16[512,8,384]{2,1,0:T(8,128)(2,1)}, u32[]{:S(2)}, u32[]{:S(2)}) %all-to-all-start.3) | async-done | bytes 3145760 | tf_op jit(solution)/shard_map/all_to_all | solution.py:578
  143.2 9.9 %all-to-all-start.2 = ((bf16[512,8,384]{2,1,0:T(8,128)(2,1)}), bf16[512,8,384]{2,1,0:T(8,128)(2,1)S(1)}, u32[]{:S(2)}, u32[]{:S(2)}) async-start(bf16[512,8,384]{2,1,0:T(8,128)(2,1)} %bitcast.26), calls=%async_computation.2 | async-start | bytes 6291456 | tf_op jit(solution)/shard_map/all_to_all | solution.py:578
  155.1 10.6 %gather_2.1.rows_ref = bf16[4096,512]{1,0:T(8,128)(2,1)} custom-call(s32[512,16]{1,0:T(8,128)} %bitcast.43, bf16[1024,768]{1,0:T(8,128)(2,1)} %refs_1_.5, bf16[8,128]{1,0:T(8,128)(2,1)} %slice.33.refs_2_), custom_call_target="tpu_custom_call" | custom-call | flops 6442450944 | bytes 4194304 | tf_op jit(solution)/shard_map/gather_2/pallas_call | solution.py:134
  165.8 6.6 %sum_slots.1.sums_ref = f32[768,384]{1,0:T(8,128)} custom-call(s32[1,4096]{1,0:T(1,128)} %reshape.43.node_ref, bf16[4096,384]{1,0:T(8,128)(2,1)} %bitcast.10.rows_ref), custom_call_target="tpu_custom_call" | custom-call | flops 2415919104 | bytes 3145728 | tf_op jit(solution)/shard_map/sum_slots/pallas_call | solution.py:183
  173.6 56.5 %all-to-all-done.2 = bf16[512,8,384]{2,1,0:T(8,128)(2,1)S(1)} async-done(((bf16[512,8,384]{2,1,0:T(8,128)(2,1)}), bf16[512,8,384]{2,1,0:T(8,128)(2,1)S(1)}, u32[]{:S(2)}, u32[]{:S(2)}) %all-to-all-start.2) | async-done | bytes 3145760 | tf_op jit(solution)/shard_map/all_to_all | solution.py:578
  231.7 2.6 ride_class.1
  234.4 12.0 %all-to-all-start.4 = ((bf16[512,8,512]{2,1,0:T(8,128)(2,1)}), bf16[512,8,512]{2,1,0:T(8,128)(2,1)}, u32[]{:S(2)}, u32[]{:S(2)}) async-start(bf16[512,8,512]{2,1,0:T(8,128)(2,1)} %bitcast.30), calls=%async_computation.4 | async-start | bytes 8388608 | tf_op jit(solution)/shard_map/all_to_all | solution.py:578
  248.9 14.1 %sum_folded.1 = (f32[768,1024]{1,0:T(8,128)}, f32[768,384]{1,0:T(8,128)}, bf16[256,768]{1,0:T(8,128)(2,1)}, f32[256,1]{1,0:T(8,128)}, f32[768,1]{1,0:T(8,128)}) custom-call(s32[1,4096]{1,0:T(1,128)} %reshape.49.node_ref, bf16[4096,384]{1,0:T(8,128)(2,1)} %bitcast.28, f32[768,384]{1,0:T(8,128)} %sum_slots.1.sums_ref, s32[1,256]{1,0:T(1,128)} %hop1_ref.3, ...), custom_call_target="tpu_custom_call" | custom-call | flops 4831838208 | bytes 3145728 | tf_op jit(solution)/shard_map/sum_folded/pallas_call | solution.py:251
  263.1 81.1 %all-to-all-done.4 = bf16[512,8,512]{2,1,0:T(8,128)(2,1)} async-done(((bf16[512,8,512]{2,1,0:T(8,128)(2,1)}), bf16[512,8,512]{2,1,0:T(8,128)(2,1)}, u32[]{:S(2)}, u32[]{:S(2)}) %all-to-all-start.4) | async-done | bytes 4194336 | tf_op jit(solution)/shard_map/all_to_all | solution.py:578
  344.1 14.9 %forward.1 = (f32[153,256]{1,0:T(8,128)}, f32[153,1024]{1,0:T(8,128)}) custom-call(s32[1,4096]{1,0:T(1,128)} %reshape.43.node_ref, s32[1,1024]{1,0:T(1,128)} %reshape.44.last_ref, bf16[4096,512]{1,0:T(8,128)(2,1)} %bitcast.12.rows_ref, f32[768,384]{1,0:T(8,128)} %get-tuple-element.29.sums_ref, f32[768,1024]{1,0:T(8,128)} %get-tuple-element.30.pre_ref, ...), custom_call_target="tpu_custom_call" | custom-call | flops 3019898880 | bytes 4194304 | tf_op jit(solution)/shard_map/forward/pallas_call | solution.py:344
  (39 shorter events, 23.5 us)
Async XLA Ops:
  55.0 88.3 %all-to-all-start.3 = ((bf16[512,8,384]{2,1,0:T(8,128)(2,1)}), bf16[512,8,384]{2,1,0:T(8,128)(2,1)}, u32[]{:S(2)}, u32[]{:S(2)}) async-start(bf16[512,8,384]{2,1,0:T(8,128)(2,1)} %bitcast.31), calls=%async_computation.3 | async-start | bytes 6291456 | tf_op jit(solution)/shard_map/all_to_all | solution.py:578
  79.4 6.3 %collective-permute-start = (f32[1024,512]{1,0:T(8,128)}, f32[1024,512]{1,0:T(8,128)S(1)}, u32[]{:S(2)}, u32[]{:S(2)}) collective-permute-start(f32[1024,512]{1,0:T(8,128)} %get-tuple-element.23), channel_id=1, source_target_pairs={{0,32},{32,0},{64,96},{96,64},{128,160},{160,128},{192,224},{224,1... | collective-permute-start | bytes 6291464 | tf_op jit(solution)/shard_map/ppermute | solution.py:452
  85.6 1.4 copy-start.6
  92.4 20.9 %collective-permute-start.1 = (bf16[1024,128]{1,0:T(8,128)(2,1)}, bf16[1024,128]{1,0:T(8,128)(2,1)S(1)}, u32[]{:S(2)}, u32[]{:S(2)}) collective-permute-start(bf16[1024,128]{1,0:T(8,128)(2,1)} %get-tuple-element.25), channel_id=1, source_target_pairs={{0,8},{1,9},{2,10},{3,11},{4,12},{5,13},{6,14},{7,15},{8,0},{9,1},... | collective-permute-start | bytes 786440 | tf_op jit(solution)/shard_map/ppermute | solution.py:452
  95.8 25.4 %collective-permute-start.2 = (bf16[1024,128]{1,0:T(8,128)(2,1)}, bf16[1024,128]{1,0:T(8,128)(2,1)S(1)}, u32[]{:S(2)}, u32[]{:S(2)}) collective-permute-start(bf16[1024,128]{1,0:T(8,128)(2,1)} %get-tuple-element.26), channel_id=1, source_target_pairs={{0,16},{1,17},{2,18},{3,19},{4,20},{5,21},{6,22},{7,23},{8,24},{9,... | collective-permute-start | bytes 786440 | tf_op jit(solution)/shard_map/ppermute | solution.py:452
  100.4 27.3 %copy-start.3 = (f32[1024,128]{1,0:T(8,128)S(1)}, f32[1024,128]{1,0:T(8,128)}, u32[]{:S(2)}) copy-start(f32[1024,128]{1,0:T(8,128)} %get-tuple-element.24.own_ref) | copy-start | bytes 1572868
  100.4 27.3 %collective-permute-start.3 = (bf16[1024,128]{1,0:T(8,128)(2,1)}, bf16[1024,128]{1,0:T(8,128)(2,1)S(1)}, u32[]{:S(2)}, u32[]{:S(2)}) collective-permute-start(bf16[1024,128]{1,0:T(8,128)(2,1)} %get-tuple-element.27), channel_id=1, source_target_pairs={{0,24},{1,25},{2,26},{3,27},{4,28},{5,29},{6,30},{7,31},{8,16},{9,... | collective-permute-start | bytes 786440 | tf_op jit(solution)/shard_map/ppermute | solution.py:452
  127.7 1.9 copy-start
  131.6 1.7 copy-start.1
  143.2 9.9 %copy-start.5 = (s32[512,16]{1,0:T(8,128)S(1)}, s32[512,16]{1,0:T(8,128)}, u32[]{:S(2)}) copy-start(s32[512,16]{1,0:T(8,128)} %get-tuple-element.20) | copy-start | bytes 98308
  143.2 86.9 %all-to-all-start.2 = ((bf16[512,8,384]{2,1,0:T(8,128)(2,1)}), bf16[512,8,384]{2,1,0:T(8,128)(2,1)S(1)}, u32[]{:S(2)}, u32[]{:S(2)}) async-start(bf16[512,8,384]{2,1,0:T(8,128)(2,1)} %bitcast.26), calls=%async_computation.2 | async-start | bytes 6291456 | tf_op jit(solution)/shard_map/all_to_all | solution.py:578
  230.1 4.3 %copy-start.2 = (bf16[512,8,384]{2,1,0:T(8,128)(2,1)}, bf16[512,8,384]{2,1,0:T(8,128)(2,1)S(1)}, u32[]{:S(2)}) copy-start(bf16[512,8,384]{2,1,0:T(8,128)(2,1)S(1)} %all-to-all-done.2) | copy-start | bytes 9437188
  230.8 1.0 copy-start.4
  234.4 109.7 %all-to-all-start.4 = ((bf16[512,8,512]{2,1,0:T(8,128)(2,1)}), bf16[512,8,512]{2,1,0:T(8,128)(2,1)}, u32[]{:S(2)}, u32[]{:S(2)}) async-start(bf16[512,8,512]{2,1,0:T(8,128)(2,1)} %bitcast.30), calls=%async_computation.4 | async-start | bytes 8388608 | tf_op jit(solution)/shard_map/all_to_all | solution.py:578

commit v4 on v3

--- a/solution.py
+++ b/solution.py
@@ -43,7 +43,8 @@
     before = (iota((step, step), 0) < iota((step, step), 1)).astype(BF16)
     owner_at = iota((DEVICES, step), 0)
     slot_at = iota((LANES_CAP, step), 0)
-    carry = jnp.zeros((DEVICES, 1), F32)
+    ones = jnp.ones((step, step), BF16)
+    carry = jnp.zeros((DEVICES, step), F32)
     total = jnp.zeros((DEVICES, 2 * LANES_CAP), F32)
     for blk in range(owner_ref.shape[1] // step):
         at = pl.ds(blk * step, step)
@@ -57,11 +58,10 @@
             )
         want = block_ref[:, at] * BLOCK_ROWS + offset_ref[:, at]
         here = owner_at == owner_ref[:, at]
-        here_f = jnp.where(here, 1.0, 0.0)
-        here_b = here_f.astype(BF16)
+        here_b = jnp.where(here, 1.0, 0.0).astype(BF16)
         seen = dot(here_b, before) + carry
         rank = jnp.sum(jnp.where(here, seen, 0.0), axis=0, keepdims=True).astype(jnp.int32)
-        carry = carry + jnp.sum(here_f, axis=1, keepdims=True)
+        carry = carry + dot(here_b, ones)
         mine = slot_at == rank
 
         def fields(part):
@@ -297,6 +297,7 @@
     acc_ref,
     pre_all,
     w1_all,
+    takes_ref,
 ):
     nodes, half = sums_ref.shape
     block = pre_ref.shape[1]
@@ -305,15 +306,21 @@
     add_up(acc_ref, dot(zero_one(taken(node_ref, nodes)), rows_ref[:, :half]))
     tile = rows_ref[:, half:]
     count = tile.shape[0]
-    shape = count // 4, count
-    j, i = iota(shape, 0), iota(shape, 1)
-    same, odd, sub = (i >> 3) == (j >> 1), j & 1, i & 7
-    last = dot(zero_one(same & (sub == odd)), tile).astype(BF16)
+
+    @pl.when(pl.program_id(0) == 0)
+    def _():
+        shape = count // 4, count
+        j, i = iota(shape, 0), iota(shape, 1)
+        same, odd, sub = (i >> 3) == (j >> 1), j & 1, i & 7
+        takes_ref[0] = zero_one(same & (sub == odd))
+        takes_ref[1] = zero_one(same & ((sub == 2 + odd) | (sub == 4 + odd)))
+        takes_ref[2] = zero_one(same & (sub == 6))
+
+    last = dot(takes_ref[0], tile).astype(BF16)
     acc_ref[:, half - PIECE :] += dot(zero_one(taken(last_ref, nodes)), last)
 
-    first = zero_one(same & ((sub == 2 + odd) | (sub == 4 + odd)))
-    class_ref[:PIECE, :] = dot(tile, first, ((0,), (1,)))
-    rest = dot(tile, zero_one(same & (sub == 6)), ((0,), (1,)))
+    class_ref[:PIECE, :] = dot(tile, takes_ref[1], ((0,), (1,)))
+    rest = dot(tile, takes_ref[2], ((0,), (1,)))
     rest = rest[:64] + rest[64:]
     more = class_ref.shape[0] - PIECE
     odd = (iota((more, count // 4), 1) & 1) == 1
@@ -368,6 +375,7 @@
             pltpu.VMEM((nodes, half), F32),
             pltpu.VMEM((steps, nodes, hid // steps), F32),
             pltpu.VMEM((steps, half, hid // steps), BF16),
+            pltpu.VMEM((3, step // 4, step), BF16),
         ],
         compiler_params=params(MOST_MIB),
         cost_estimate=pl.CostEstimate(

time: 360 us -> 359 us (level)
  no operation moved by 1% of the time
where the time goes in v4:
time: 359 us; the launch traced here: 358 us
  waiting for transfers between devices  166 us (46%)
  Pallas kernels  89.4 us (25%)
  starting transfers between devices  47.6 us (13%)
  blocking collectives  35.7 us (10%)
  local copies, waits for them, and re-layouts  17.2 us (5%)
    all_to_all x3, waiting for transfers between devices, exchange(): return lax.all_to_all(rows, BOTH, split_axis=0, concat_axis=0, tiled=True)  147 us
    all_to_all x3, starting transfers between devices, exchange(): return lax.all_to_all(rows, BOTH, split_axis=0, concat_axis=0, tiled=True)  34.8 us
    pallas_call x3, Pallas kernels, gather(): pl.pallas_call(lambda *refs: gather_kernel(part, *refs), grid=(DEVICES //...  28.2 us
    ppermute x4, waiting for transfers between devices, swap(): return lax.ppermute(rows, axis, [(i, i ^ bit) for i in range(size)])  18.5 us
    all_to_all x1, blocking collectives, on_device(): lax.all_to_all(want.reshape(outer, inner, LANES_CAP), 'gx', split_axis=0,...  17.9 us
    all_to_all x1, blocking collectives, on_device(): lax.all_to_all(lax.all_to_all(want.reshape(outer, inner, LANES_CAP), 'gx'...  17.8 us
    pallas_call x1, Pallas kernels, forward(): pl.pallas_call(forward_kernel, grid=(steps,), in_specs=[pl.BlockSpec((1,...  15.2 us
    pallas_call x1, Pallas kernels, sum_folded(): pl.pallas_call(sum_folded_kernel, grid=(count // step,), in_specs=[pl.Blo...  14.1 us
  transfers between devices with their start and end apart: 7, of which 6 were waited for; matrix products, arithmetic and copies ran while one was open for 2% of the time, Pallas kernels for 16%

profile of v4, /device:TPU:16, one launch (start us, length us, event | category | flops | bytes accessed | tf_op | source)
XLA Modules:
  0.0 358.3 jit_solution(9851817573014598251)
XLA Ops:
  0.6 5.7 %route.1 = (s32[512,16]{1,0:T(8,128)}, s32[512,16]{1,0:T(8,128)}) custom-call(s32[1,3072]{1,0:T(1,128)} %bitcast.48, s32[1,3072]{1,0:T(1,128)} %block_ref.1, s32[1,3072]{1,0:T(1,128)} %offset_ref.1, s32[1,768]{1,0:T(1,128)} %hop2_ref.3), custom_call_target="tpu_custom_call" | custom-call | flops 4000000000 | bytes 200000 | tf_op jit(solution)/shard_map/route/pallas_call | solution.py:85
  7.5 17.9 %all_to_all.43 = s32[16,1,512]{2,1,0:T(1,128)S(1)} all-to-all(s32[16,1,512]{2,1,0:T(1,128)S(1)} %reshape.52), channel_id=1, replica_groups=mesh['gx'=16,'gy'=32] {'gx'}, dimensions={0} | all-to-all | bytes 65536 | tf_op jit(solution)/shard_map/all_to_all | solution.py:605
  27.1 17.8 %all_to_all.44 = s32[32,1,256]{2,1,0:T(1,128)S(1)} all-to-all(s32[32,1,256]{2,1,0:T(1,128)S(1)} %reshape.54), channel_id=1, replica_groups=mesh['gx'=16,'gy'=32] {'gy'}, dimensions={0} | all-to-all | bytes 65536 | tf_op jit(solution)/shard_map/all_to_all | solution.py:604
  46.5 7.4 %gather_0.1 = bf16[4096,384]{1,0:T(8,128)(2,1)} custom-call(s32[512,16]{1,0:T(8,128)} %bitcast.40, bf16[1024,768]{1,0:T(8,128)(2,1)} %refs_1_.5, s32[512,16]{1,0:T(8,128)} %bitcast.41), custom_call_target="tpu_custom_call" | custom-call | flops 3221225472 | bytes 3145728 | tf_op jit(solution)/shard_map/gather_0/pallas_call | solution.py:134
  53.9 13.0 %all-to-all-start.3 = ((bf16[512,8,384]{2,1,0:T(8,128)(2,1)}), bf16[512,8,384]{2,1,0:T(8,128)(2,1)}, u32[]{:S(2)}, u32[]{:S(2)}) async-start(bf16[512,8,384]{2,1,0:T(8,128)(2,1)} %bitcast.31), calls=%async_computation.3 | async-start | bytes 6291456 | tf_op jit(solution)/shard_map/all_to_all | solution.py:586
  68.2 10.1 %backward.1 = (f32[1024,512]{1,0:T(8,128)}, f32[1024,512]{1,0:T(8,128)}) custom-call(s32[1]{0:T(128)} %bitcast.2.core_ref, bf16[768,768]{1,0:T(8,128)(2,1)} %agg_ref.1, s32[1,256]{1,0:T(1,128)} %hop1_ref.2, bf16[153,256]{1,0:T(8,128)(2,1)} %bitcast.47, bf16[768,1024]{1,0:T(8,128)(2,1)} %w1_ref.5, bf16[153,1024]{1,0:T(8,128)(2,1)} %bitcast.37, ...), custom_call_target="tpu_custom_call" | custom-call | flops 2415919104 | bytes 6291456 | tf_op jit(solution)/shard_map/backward/pallas_call | solution.py:436
  80.4 4.2 %collective-permute-done.got_ref = f32[1024,512]{1,0:T(8,128)S(1)} collective-permute-done((f32[1024,512]{1,0:T(8,128)}, f32[1024,512]{1,0:T(8,128)S(1)}, u32[]{:S(2)}, u32[]{:S(2)}) %collective-permute-start) | collective-permute-done | bytes 2097184 | tf_op jit(solution)/shard_map/ppermute | solution.py:460
  85.9 4.1 %split.1 = (f32[1024,128]{1,0:T(8,128)}, bf16[1024,128]{1,0:T(8,128)(2,1)}, bf16[1024,128]{1,0:T(8,128)(2,1)}, bf16[1024,128]{1,0:T(8,128)(2,1)}) custom-call(s32[1]{0:T(128)} %bitcast.1.x_ref, f32[1024,512]{1,0:T(8,128)} %get-tuple-element.22.kept_ref, f32[1024,512]{1,0:T(8,128)} %copy-done.6), custom_call_target="tpu_custom_call" | custom-call | tf_op jit(solution)/shard_map/split/pallas_call | solution.py:478
  91.3 3.4 collective-permute-start.1
  94.7 4.6 %collective-permute-start.2 = (bf16[1024,128]{1,0:T(8,128)(2,1)}, bf16[1024,128]{1,0:T(8,128)(2,1)S(1)}, u32[]{:S(2)}, u32[]{:S(2)}) collective-permute-start(bf16[1024,128]{1,0:T(8,128)(2,1)} %get-tuple-element.26), channel_id=1, source_target_pairs={{0,16},{1,17},{2,18},{3,19},{4,20},{5,21},{6,22},{7,23},{8,24},{9,... | collective-permute-start | bytes 786440 | tf_op jit(solution)/shard_map/ppermute | solution.py:460
  99.4 2.7 collective-permute-start.3
  102.1 10.2 %gather_1.1.refs_3_ = bf16[4096,384]{1,0:T(8,128)(2,1)} custom-call(s32[512,16]{1,0:T(8,128)} %bitcast.42, bf16[1024,768]{1,0:T(8,128)(2,1)} %refs_1_.5, f32[8,128]{1,0:T(8,128)} %slice.27.refs_2_), custom_call_target="tpu_custom_call" | custom-call | flops 6442450944 | bytes 3145728 | tf_op jit(solution)/shard_map/gather_1/pallas_call | solution.py:134
  112.3 7.8 %collective-permute-done.2.refs_1_ = bf16[1024,128]{1,0:T(8,128)(2,1)S(1)} collective-permute-done((bf16[1024,128]{1,0:T(8,128)(2,1)}, bf16[1024,128]{1,0:T(8,128)(2,1)S(1)}, u32[]{:S(2)}, u32[]{:S(2)}) %collective-permute-start.2) | collective-permute-done | bytes 262176 | tf_op jit(solution)/shard_map/ppermute | solution.py:460
  120.1 6.5 %collective-permute-done.3.refs_2_ = bf16[1024,128]{1,0:T(8,128)(2,1)S(1)} collective-permute-done((bf16[1024,128]{1,0:T(8,128)(2,1)}, bf16[1024,128]{1,0:T(8,128)(2,1)S(1)}, u32[]{:S(2)}, u32[]{:S(2)}) %collective-permute-start.3) | collective-permute-done | bytes 262176 | tf_op jit(solution)/shard_map/ppermute | solution.py:460
  132.3 9.9 %all-to-all-done.3 = bf16[512,8,384]{2,1,0:T(8,128)(2,1)} async-done(((bf16[512,8,384]{2,1,0:T(8,128)(2,1)}), bf16[512,8,384]{2,1,0:T(8,128)(2,1)}, u32[]{:S(2)}, u32[]{:S(2)}) %all-to-all-start.3) | async-done | bytes 3145760 | tf_op jit(solution)/shard_map/all_to_all | solution.py:586
  142.2 9.9 %all-to-all-start.2 = ((bf16[512,8,384]{2,1,0:T(8,128)(2,1)}), bf16[512,8,384]{2,1,0:T(8,128)(2,1)S(1)}, u32[]{:S(2)}, u32[]{:S(2)}) async-start(bf16[512,8,384]{2,1,0:T(8,128)(2,1)} %bitcast.26), calls=%async_computation.2 | async-start | bytes 6291456 | tf_op jit(solution)/shard_map/all_to_all | solution.py:586
  154.1 10.6 %gather_2.1.rows_ref = bf16[4096,512]{1,0:T(8,128)(2,1)} custom-call(s32[512,16]{1,0:T(8,128)} %bitcast.43, bf16[1024,768]{1,0:T(8,128)(2,1)} %refs_1_.5, bf16[8,128]{1,0:T(8,128)(2,1)} %slice.33.refs_2_), custom_call_target="tpu_custom_call" | custom-call | flops 6442450944 | bytes 4194304 | tf_op jit(solution)/shard_map/gather_2/pallas_call | solution.py:134
  164.7 6.6 %sum_slots.1.sums_ref = f32[768,384]{1,0:T(8,128)} custom-call(s32[1,4096]{1,0:T(1,128)} %reshape.43.node_ref, bf16[4096,384]{1,0:T(8,128)(2,1)} %bitcast.10.rows_ref), custom_call_target="tpu_custom_call" | custom-call | flops 2415919104 | bytes 3145728 | tf_op jit(solution)/shard_map/sum_slots/pallas_call | solution.py:183
  172.6 56.5 %all-to-all-done.2 = bf16[512,8,384]{2,1,0:T(8,128)(2,1)S(1)} async-done(((bf16[512,8,384]{2,1,0:T(8,128)(2,1)}), bf16[512,8,384]{2,1,0:T(8,128)(2,1)S(1)}, u32[]{:S(2)}, u32[]{:S(2)}) %all-to-all-start.2) | async-done | bytes 3145760 | tf_op jit(solution)/shard_map/all_to_all | solution.py:586
  230.7 2.6 ride_class.1
  233.3 12.0 %all-to-all-start.4 = ((bf16[512,8,512]{2,1,0:T(8,128)(2,1)}), bf16[512,8,512]{2,1,0:T(8,128)(2,1)}, u32[]{:S(2)}, u32[]{:S(2)}) async-start(bf16[512,8,512]{2,1,0:T(8,128)(2,1)} %bitcast.30), calls=%async_computation.4 | async-start | bytes 8388608 | tf_op jit(solution)/shard_map/all_to_all | solution.py:586
  247.9 14.1 %sum_folded.1 = (f32[768,1024]{1,0:T(8,128)}, f32[768,384]{1,0:T(8,128)}, bf16[256,768]{1,0:T(8,128)(2,1)}, f32[256,1]{1,0:T(8,128)}, f32[768,1]{1,0:T(8,128)}) custom-call(s32[1,4096]{1,0:T(1,128)} %reshape.49.node_ref, bf16[4096,384]{1,0:T(8,128)(2,1)} %bitcast.28, f32[768,384]{1,0:T(8,128)} %sum_slots.1.sums_ref, s32[1,256]{1,0:T(1,128)} %hop1_ref.3, ...), custom_call_target="tpu_custom_call" | custom-call | flops 4831838208 | bytes 3145728 | tf_op jit(solution)/shard_map/sum_folded/pallas_call | solution.py:251
  262.0 81.1 %all-to-all-done.4 = bf16[512,8,512]{2,1,0:T(8,128)(2,1)} async-done(((bf16[512,8,512]{2,1,0:T(8,128)(2,1)}), bf16[512,8,512]{2,1,0:T(8,128)(2,1)}, u32[]{:S(2)}, u32[]{:S(2)}) %all-to-all-start.4) | async-done | bytes 4194336 | tf_op jit(solution)/shard_map/all_to_all | solution.py:586
  343.1 15.2 %forward.1 = (f32[153,256]{1,0:T(8,128)}, f32[153,1024]{1,0:T(8,128)}) custom-call(s32[1,4096]{1,0:T(1,128)} %reshape.43.node_ref, s32[1,1024]{1,0:T(1,128)} %reshape.44.last_ref, bf16[4096,512]{1,0:T(8,128)(2,1)} %bitcast.12.rows_ref, f32[768,384]{1,0:T(8,128)} %get-tuple-element.29.sums_ref, f32[768,1024]{1,0:T(8,128)} %get-tuple-element.30.pre_ref, ...), custom_call_target="tpu_custom_call" | custom-call | flops 3019898880 | bytes 4194304 | tf_op jit(solution)/shard_map/forward/pallas_call | solution.py:351
  (39 shorter events, 23.5 us)
Async XLA Ops:
  53.9 88.3 %all-to-all-start.3 = ((bf16[512,8,384]{2,1,0:T(8,128)(2,1)}), bf16[512,8,384]{2,1,0:T(8,128)(2,1)}, u32[]{:S(2)}, u32[]{:S(2)}) async-start(bf16[512,8,384]{2,1,0:T(8,128)(2,1)} %bitcast.31), calls=%async_computation.3 | async-start | bytes 6291456 | tf_op jit(solution)/shard_map/all_to_all | solution.py:586
  78.3 6.3 %collective-permute-start = (f32[1024,512]{1,0:T(8,128)}, f32[1024,512]{1,0:T(8,128)S(1)}, u32[]{:S(2)}, u32[]{:S(2)}) collective-permute-start(f32[1024,512]{1,0:T(8,128)} %get-tuple-element.23), channel_id=1, source_target_pairs={{0,32},{32,0},{64,96},{96,64},{128,160},{160,128},{192,224},{224,1... | collective-permute-start | bytes 6291464 | tf_op jit(solution)/shard_map/ppermute | solution.py:460
  84.5 1.4 copy-start.6
  91.3 20.9 %collective-permute-start.1 = (bf16[1024,128]{1,0:T(8,128)(2,1)}, bf16[1024,128]{1,0:T(8,128)(2,1)S(1)}, u32[]{:S(2)}, u32[]{:S(2)}) collective-permute-start(bf16[1024,128]{1,0:T(8,128)(2,1)} %get-tuple-element.25), channel_id=1, source_target_pairs={{0,8},{1,9},{2,10},{3,11},{4,12},{5,13},{6,14},{7,15},{8,0},{9,1},... | collective-permute-start | bytes 786440 | tf_op jit(solution)/shard_map/ppermute | solution.py:460
  94.7 25.4 %collective-permute-start.2 = (bf16[1024,128]{1,0:T(8,128)(2,1)}, bf16[1024,128]{1,0:T(8,128)(2,1)S(1)}, u32[]{:S(2)}, u32[]{:S(2)}) collective-permute-start(bf16[1024,128]{1,0:T(8,128)(2,1)} %get-tuple-element.26), channel_id=1, source_target_pairs={{0,16},{1,17},{2,18},{3,19},{4,20},{5,21},{6,22},{7,23},{8,24},{9,... | collective-permute-start | bytes 786440 | tf_op jit(solution)/shard_map/ppermute | solution.py:460
  99.4 27.3 %copy-start.3 = (f32[1024,128]{1,0:T(8,128)S(1)}, f32[1024,128]{1,0:T(8,128)}, u32[]{:S(2)}) copy-start(f32[1024,128]{1,0:T(8,128)} %get-tuple-element.24.own_ref) | copy-start | bytes 1572868
  99.4 27.3 %collective-permute-start.3 = (bf16[1024,128]{1,0:T(8,128)(2,1)}, bf16[1024,128]{1,0:T(8,128)(2,1)S(1)}, u32[]{:S(2)}, u32[]{:S(2)}) collective-permute-start(bf16[1024,128]{1,0:T(8,128)(2,1)} %get-tuple-element.27), channel_id=1, source_target_pairs={{0,24},{1,25},{2,26},{3,27},{4,28},{5,29},{6,30},{7,31},{8,16},{9,... | collective-permute-start | bytes 786440 | tf_op jit(solution)/shard_map/ppermute | solution.py:460
  126.6 1.9 copy-start
  130.6 1.7 copy-start.1
  142.2 9.9 %copy-start.5 = (s32[512,16]{1,0:T(8,128)S(1)}, s32[512,16]{1,0:T(8,128)}, u32[]{:S(2)}) copy-start(s32[512,16]{1,0:T(8,128)} %get-tuple-element.20) | copy-start | bytes 98308
  142.2 86.9 %all-to-all-start.2 = ((bf16[512,8,384]{2,1,0:T(8,128)(2,1)}), bf16[512,8,384]{2,1,0:T(8,128)(2,1)S(1)}, u32[]{:S(2)}, u32[]{:S(2)}) async-start(bf16[512,8,384]{2,1,0:T(8,128)(2,1)} %bitcast.26), calls=%async_computation.2 | async-start | bytes 6291456 | tf_op jit(solution)/shard_map/all_to_all | solution.py:586
  229.0 4.3 %copy-start.2 = (bf16[512,8,384]{2,1,0:T(8,128)(2,1)}, bf16[512,8,384]{2,1,0:T(8,128)(2,1)S(1)}, u32[]{:S(2)}) copy-start(bf16[512,8,384]{2,1,0:T(8,128)(2,1)S(1)} %all-to-all-done.2) | copy-start | bytes 9437188
  229.7 1.0 copy-start.4
  233.3 109.7 %all-to-all-start.4 = ((bf16[512,8,512]{2,1,0:T(8,128)(2,1)}), bf16[512,8,512]{2,1,0:T(8,128)(2,1)}, u32[]{:S(2)}, u32[]{:S(2)}) async-start(bf16[512,8,512]{2,1,0:T(8,128)(2,1)} %bitcast.30), calls=%async_computation.4 | async-start | bytes 8388608 | tf_op jit(solution)/shard_map/all_to_all | solution.py:586
